TPU v7x, 32 devices: a whole 2x2x4 slice. The times are simulated.
32 devices in a mesh: ty: 8 (over y, x, core), tx: 4 (over z).
Axes of the slice: x: 2, y: 2, z: 4, core: 2. Of those that a mesh axis runs over, the one named last changes fastest.
Arguments:
- object_field: float32 [2, 2048, 1024], P(None, 'ty', 'tx'), may hold values from -6 to 6
- probe_modes: float32 [2, 2, 256, 256], replicated, may hold values from -6 to 6
- intensities: float32 [8, 4, 3, 256, 256], P('ty', 'tx'), may hold values from 0.25 to 16
- offsets: int32 [8, 4, 3, 2], P('ty', 'tx'), may hold values from 0 to 256
- counts: int32 [8, 4], replicated, may hold values from 1 to 3, as said below
Outputs:
- object_grad: float32 [2, 2048, 1024], P(None, 'ty', 'tx')
- probe_grad: float32 [2, 2, 256, 256], replicated
Inputs may be any that keep to these rules, and one draw needn't show every extreme that they name: Tile (a, b) uses slots 0 to counts[a, b] - 1 of intensities and offsets; its other slots are ignored. In every draw some tile uses all 3 slots.
All inputs are finite; a program needn't handle non-finite values.
Results may differ from a plain program's by a relative error of at most 0.0003.
Values sent between devices are 32-bit elements; how exact they have to be, the bound alone decides.
No kernel may reach another device: no remote copies, remote signals or barrier semaphores. Data moves between devices by JAX's collectives and lax.ppermute only.
A program may use at most 64 MiB of HBM per device.

v0:
```python
import functools
import math

import jax
import jax.numpy as jnp
import ml_dtypes
import numpy as np
from jax import lax
from jax.experimental import pallas as pl
from jax.experimental.pallas import tpu as pltpu
from jax.sharding import PartitionSpec as P

FLOOR = 0.5
LANES = 128
CHUNK = 32
HEAVY = 0
AHEAD = 4_000_000_000
AROUND = 2_000_000_000
VMEM_LIMIT = 28 * 1024 * 1024
SMALL_LIMIT = 8 * 1024 * 1024


def split_table(table):
    high = table.astype(ml_dtypes.bfloat16)
    low = (table - high.astype(np.float64)).astype(ml_dtypes.bfloat16)
    return high, low


def complex_block(matrix):
    return np.block([[matrix.real, matrix.imag], [-matrix.imag, matrix.real]])


@functools.lru_cache(maxsize=None)
def fourier_tables(pattern):
    half = pattern // 2
    n = np.arange(half)
    tables = []
    for parity in (0, 1):
        k = 2 * np.arange(half) + parity
        tables.append(np.exp(-2j * np.pi * ((n[:, None] * k[None, :]) % pattern) / pattern) / math.sqrt(pattern))
    forward = [complex_block(t) for t in tables]
    inverse = [complex_block(np.conj(t).T) for t in tables]
    every = forward + [t.T for t in forward] + [t.T for t in inverse] + inverse
    return np.stack([np.stack(split_table(t)) for t in every])


def split(value):
    high = value.astype(jnp.bfloat16)
    low = (value - high.astype(jnp.float32)).astype(jnp.bfloat16)
    return high, low


def mul(a, b):
    return jnp.dot(a, b, preferred_element_type=jnp.float32)


def near_and_far(unit):
    odd = lax.axis_index("ty") % 2
    return pl.multiple_of((1 - odd) * unit, LANES), pl.multiple_of(odd * unit, LANES)


def inner_and_outer():
    odd = lax.axis_index("tx") % 2
    return pl.multiple_of((1 - odd) * LANES, LANES), pl.multiple_of(odd * LANES, LANES)


def edges_kernel(field, center, chip_rows, inner_side, outer_side, sems):
    _, far = near_and_far(LANES)
    inner, outer = inner_and_outer()
    moves = (
        (field.at[:, pl.ds(far, LANES), :], chip_rows),
        (field.at[:, :, pl.ds(inner, LANES)], inner_side),
        (field.at[:, :, pl.ds(outer, LANES)], outer_side),
        (field, center),
    )
    copies = [pltpu.make_async_copy(source, target, sems.at[i]) for i, (source, target) in enumerate(moves)]
    for copy in copies:
        copy.start()
    for copy in copies:
        copy.wait()


def near_kernel(inner_side, outer_side, inner_near, outer_near):
    near, _ = near_and_far(LANES)
    inner_near[...] = inner_side[:, pl.ds(near, LANES), :]
    outer_near[...] = outer_side[:, pl.ds(near, LANES), :]


def far_kernel(chip_rows, inner_corner, outer_corner, far_rows):
    inner = (1 - lax.axis_index("tx") % 2) * 3
    for b in range(2):
        far_rows[:, 1 + b] = chip_rows[:, :, b * LANES : (b + 1) * LANES]
    far_rows[:, inner] = inner_corner[...]
    far_rows[:, 3 - inner] = outer_corner[...]


def corners_kernel(chip_rows, _, __, inner_corner, outer_corner):
    for target, start in zip((inner_corner, outer_corner), inner_and_outer()):
        target[...] = chip_rows[:, :, pl.ds(start, LANES)]


def root_kernel(measured, root, halves):
    pattern = measured.shape[2]
    source = lax.broadcasted_iota(jnp.int32, (pattern, pattern), 0)
    place = lax.broadcasted_iota(jnp.int32, (pattern, pattern), 1)
    half = pattern // 2
    wanted = jnp.where(place < half, 2 * place, 2 * (place - half) + 1)
    order = jnp.where(source == wanted, 1.0, 0.0).astype(jnp.bfloat16)
    for slot in range(measured.shape[0]):
        for b in range(2):
            halves[slot, b] = jnp.sqrt(measured[slot, :, b * LANES : (b + 1) * LANES])
        for parity in range(2):
            rows = pl.ds(parity, LANES, stride=2)
            high, low = split(jnp.concatenate([halves[slot, 0, rows, :], halves[slot, 1, rows, :]], axis=1))
            root[slot, parity] = mul(high, order) + mul(low, order)


def places_kernel(counts, spots, scalars):
    scalars[0] = counts[lax.axis_index("tx"), lax.axis_index("ty")]
    for slot in range(spots.shape[1]):
        for axis in range(2):
            scalars[1 + 2 * slot + axis] = spots[axis, slot]


def slots_kernel(
    scalars, center, core_tile, far_rows, inner_side, outer_side, inner_near, outer_near, probe, root, tables,
    probe_sent, probe_keep, inner_side_out, outer_side_out, grad_mid,
    pad, grid, patch, rows_high, rows_low, freq, sums,
):
    half = LANES
    modes = probe.shape[1]
    length = center.shape[1]
    margin = far_rows.shape[2]
    near, far = near_and_far(margin + length)
    near, far, own = pl.ds(near, margin), pl.ds(far, margin), pl.ds(margin, length)
    core_half = pl.ds(pl.multiple_of(lax.axis_index("ty") % 2 * half, half), half)
    inner = (1 - lax.axis_index("tx") % 2) * 3
    outer = 3 - inner

    for b in range(2):
        cols = slice(b * half, (b + 1) * half)
        pad[:, 1 + b, margin : margin + length, :] = center[:, :, cols]
        pad[:, 1 + b, near, :] = core_tile[:, core_half, cols]
    pad[:, inner, own, :] = inner_side[...]
    pad[:, outer, own, :] = outer_side[...]
    pad[:, inner, near, :] = inner_near[...]
    pad[:, outer, near, :] = outer_near[...]
    pad[:, :, far, :] = far_rows[...]
    grid[...] = jnp.zeros_like(grid)
    sums[...] = jnp.zeros_like(sums)
    lane = lax.broadcasted_iota(jnp.int32, (CHUNK, half), 1)

    def slot_step(slot, carry):
        row0 = scalars[1 + 2 * slot]
        col0 = scalars[2 + 2 * slot]
        block = jnp.minimum(col0 // half, 1)
        shift = col0 - block * half
        back_shift = lax.rem(half - shift, half)
        fore_shift = lax.rem(shift, half)

        for chunk in range(half // CHUNK):
            spectra = []
            for part in range(2):
                rows = part * half + chunk * CHUNK
                here = slice(rows, rows + CHUNK)
                cells = []
                for c in range(2):
                    rolled = [
                        pltpu.roll(pad[c, block + b, pl.ds(row0 + rows, CHUNK), :], back_shift, 1) for b in range(3)
                    ]
                    for b in range(2):
                        cell = jnp.where(lane < half - shift, rolled[b], rolled[b + 1])
                        patch[c, b, here, :] = cell
                        cells.append(cell)
                lefts = []
                for m in range(modes):
                    waves = []
                    for b in range(2):
                        pr = probe[0, m, here, b * half : (b + 1) * half]
                        pi = probe[1, m, here, b * half : (b + 1) * half]
                        waves.append((pr * cells[b] - pi * cells[2 + b], pr * cells[2 + b] + pi * cells[b]))
                    (ra, ia), (rb, ib) = waves
                    lefts.append((jnp.concatenate([ra + rb, ia + ib], axis=1), jnp.concatenate([ra - rb, ia - ib], axis=1)))
                spectra.append(lefts)
            for parity in range(2):
                stacked = jnp.concatenate([spectra[part][m][parity] for m in range(modes) for part in range(2)], axis=0)
                high, low = split(stacked)
                out = mul(jnp.concatenate([high, low, high], axis=1), jnp.concatenate([tables[parity, 0], tables[parity, 0], tables[parity, 1]], axis=0))
                for m in range(modes):
                    a = out[(2 * m) * CHUNK : (2 * m + 1) * CHUNK]
                    b = out[(2 * m + 1) * CHUNK : (2 * m + 2) * CHUNK]
                    for row_parity, value in enumerate((a + b, a - b)):
                        vh, vl = split(value)
                        for c in range(2):
                            at = slice(c * half + chunk * CHUNK, c * half + (chunk + 1) * CHUNK)
                            to = slice(parity * half, (parity + 1) * half)
                            rows_high[m, row_parity, at, to] = vh[:, c * half : (c + 1) * half]
                            rows_low[m, row_parity, at, to] = vl[:, c * half : (c + 1) * half]

        def row_transform(table, parity):
            for m in range(modes):
                high = rows_high[m, parity]
                low = rows_low[m, parity]
                freq[m, parity] = mul(
                    jnp.concatenate([tables[table + parity, 0], tables[table + parity, 1], tables[table + parity, 0]], axis=1),
                    jnp.concatenate([high, high, low], axis=0),
                )

        def apply_factor(parity):
            for chunk in range(half // CHUNK):
                real = slice(chunk * CHUNK, (chunk + 1) * CHUNK)
                imag = slice(half + chunk * CHUNK, half + (chunk + 1) * CHUNK)
                values = [(freq[m, parity, real, :], freq[m, parity, imag, :]) for m in range(modes)]
                power = sum(re * re + im * im for re, im in values)
                factor = 1.0 - root[slot, parity, real, :] * lax.rsqrt(jnp.maximum(power, FLOOR * FLOOR))
                for m in range(modes):
                    for at, value in zip((real, imag), values[m]):
                        vh, vl = split(value * factor)
                        rows_high[m, parity, at, :] = vh
                        rows_low[m, parity, at, :] = vl

        row_transform(2, 0)
        row_transform(2, 1)
        apply_factor(0)
        row_transform(4, 0)
        apply_factor(1)
        row_transform(4, 1)

        for chunk in range(half // CHUNK):
            real = slice(chunk * CHUNK, (chunk + 1) * CHUNK)
            imag = slice(half + chunk * CHUNK, half + (chunk + 1) * CHUNK)
            backs = []
            for q in range(2):
                cols = slice(q * half, (q + 1) * half)
                pieces = []
                for m in range(modes):
                    even = jnp.concatenate([freq[m, 0, real, cols], freq[m, 0, imag, cols]], axis=1)
                    odd = jnp.concatenate([freq[m, 1, real, cols], freq[m, 1, imag, cols]], axis=1)
                    pieces += [even + odd, even - odd]
                high, low = split(jnp.concatenate(pieces, axis=0))
                backs.append(mul(jnp.concatenate([high, low, high], axis=1), jnp.concatenate([tables[6 + q, 0], tables[6 + q, 0], tables[6 + q, 1]], axis=0)))
            halves = (backs[0] + backs[1], backs[0] - backs[1])
            for part in range(2):
                rows = part * half + chunk * CHUNK
                here = slice(rows, rows + CHUNK)
                total = [[0.0, 0.0], [0.0, 0.0]]
                for b in range(2):
                    xr = patch[0, b, here, :]
                    xi = patch[1, b, here, :]
                    for m in range(modes):
                        at = (2 * m + part) * CHUNK
                        br = halves[b][at : at + CHUNK, :half]
                        bi = halves[b][at : at + CHUNK, half:]
                        pr = probe[0, m, here, b * half : (b + 1) * half]
                        pi = probe[1, m, here, b * half : (b + 1) * half]
                        total[0][b] += pr * br + pi * bi
                        total[1][b] += pr * bi - pi * br
                        sums[pl.ds(((b * 2 + 0) * modes + m) * length + rows, CHUNK), :] += xr * br + xi * bi
                        sums[pl.ds(((b * 2 + 1) * modes + m) * length + rows, CHUNK), :] += xr * bi - xi * br
                for c in range(2):
                    ra = pltpu.roll(total[c][0], fore_shift, 1)
                    rb = pltpu.roll(total[c][1], fore_shift, 1)
                    beyond = lane >= shift
                    zero = jnp.zeros_like(ra)
                    placed = (jnp.where(beyond, ra, zero), jnp.where(beyond, rb, ra), jnp.where(beyond, zero, rb))
                    for b in range(3):
                        grid[c, block + b, pl.ds(row0 + rows, CHUNK), :] += placed[b]
        return carry

    lax.fori_loop(0, scalars[0], slot_step, 0)

    kept, rows, _ = probe_keep.shape
    code = own_code(digit_groups())

    def place_piece(place, carry):
        for first, target in ((0, probe_keep), (kept, probe_sent)):
            piece = (place + first) ^ code
            target[place] = sums[pl.ds(pl.multiple_of(piece * rows, rows), rows), :]
        return carry

    lax.fori_loop(0, kept, place_piece, 0)
    inner_side_out[...] = grid[:, inner]
    outer_side_out[...] = grid[:, outer]
    for b in range(2):
        grad_mid[:, :, b * half : (b + 1) * half] = grid[:, 1 + b]


def rows_kernel(grad_mid, inner_side, outer_side, _, core_out, chip_out, inner_grad):
    margin, length = core_out.shape[1], inner_grad.shape[1]
    near, far = (pl.ds(start, margin) for start in near_and_far(margin + length))
    for side, start in zip((inner_side, outer_side), inner_and_outer()):
        cols = pl.ds(start, LANES)
        for target, rows in ((core_out, near), (chip_out, far), (inner_grad, slice(margin, margin + length))):
            target[:, :, cols] = grad_mid[:, rows, cols] + side[:, rows, :]


def columns_kernel(inner_grad, core_in, chip_in, grad):
    near, far = (pl.ds(start, LANES) for start in near_and_far(LANES))
    grad[:, near, :] = inner_grad[:, near, :] + core_in[...]
    grad[:, far, :] = inner_grad[:, far, :] + chip_in[...]


def after_kernel(_, *refs):
    join_pieces(refs[:-1], refs[-1])


def join_pieces(pieces, joined):
    count = pieces[0].shape[0]
    for i, piece in enumerate(pieces):
        joined[i * count : (i + 1) * count] = piece[...]


def join_kernel(first, *refs):
    source, out, sems = refs[0], refs[-2], refs[-1]
    kept, rows, _ = source.shape
    _, modes, length, _ = out.shape
    code = own_code(digit_groups())
    each = length // rows
    copies = []
    for place in range(kept):
        piece = (place + first) ^ code
        row = pl.multiple_of(piece % each * rows, rows)
        m = piece // each % modes
        c = piece // (each * modes) % 2
        b = pl.multiple_of(piece // (each * modes * 2) * LANES, LANES)
        copies.append(
            pltpu.make_async_copy(source.at[place], out.at[c, m, pl.ds(row, rows), pl.ds(b, LANES)], sems.at[place])
        )
    for copy in copies:
        copy.start()
    for copy in copies:
        copy.wait()


def exchanged(value, axis, mask):
    return lax.ppermute(value, axis, [(i, i ^ mask) for i in range(lax.axis_size(axis))])


def digit_groups():
    groups = [("ty", [1])]
    bits = [1 << i for i in range(1, lax.axis_size("ty").bit_length() - 1)]
    groups += [("ty", bits[i : i + 2]) for i in range(0, len(bits), 2)]
    return groups + [("tx", [1])]


def masks(bits):
    return [sum(bit for i, bit in enumerate(reversed(bits)) if j >> i & 1) for j in range(1 << len(bits))]


def own_code(groups):
    code = 0
    for axis, bits in groups:
        index = lax.axis_index(axis)
        for bit in bits:
            code = code * 2 + (index // bit) % 2
    return code


def pair_partner(index, kind):
    return index ^ 1 if kind == "inner" else index + 1 if index % 2 else index - 1


def paired(value, axis, kind):
    count = lax.axis_size(axis)
    pairs = [(i, pair_partner(i, kind)) for i in range(count)]
    return lax.ppermute(value, axis, [(i, j) for i, j in pairs if 0 <= j < count])


def add_kernel(scale, own, *refs):
    others, out = refs[:-1], refs[-1]
    count = out.shape[0]
    total = own[:count]
    for other in others:
        total += other[...]
    out[...] = total * scale


def added(own, others, scale=1.0, weight=0):
    out = jax.ShapeDtypeStruct(others[0].shape, jnp.float32)
    (result,) = call(functools.partial(add_kernel, scale), "add", [out], (own, *others), weight=weight)
    return result


def scattered(value, axis, bits):
    places = masks(bits)
    count = value.shape[0] // len(places)
    return [exchanged(value[j * count : (j + 1) * count], axis, places[j]) for j in range(1, len(places))]


def gathered(value, axis, bits):
    return [value] + [exchanged(value, axis, mask) for mask in masks(bits)[1:]]


def call(body, name, out, operands, spaces="", results="", scratch=(), limit=SMALL_LIMIT, weight=0, aliases=None):
    kinds = {"v": pltpu.VMEM, "s": pltpu.SMEM, "h": pltpu.HBM}

    def specs(letters, count):
        return tuple(pl.BlockSpec(memory_space=kinds[x]) for x in letters + "v" * (count - len(letters)))

    moved = sum(math.prod(v.shape) * v.dtype.itemsize for v in tuple(operands) + tuple(out))
    return pl.pallas_call(
        body,
        out_shape=tuple(out),
        in_specs=specs(spaces, len(operands)),
        out_specs=specs(results, len(out)),
        scratch_shapes=list(scratch),
        input_output_aliases=aliases or {},
        compiler_params=pltpu.CompilerParams(vmem_limit_bytes=limit),
        cost_estimate=pl.CostEstimate(flops=weight, bytes_accessed=moved, transcendentals=0),
        name=name,
    )(*operands)


def shards(object_field, probe_modes, intensities, offsets, counts):
    length = object_field.shape[1]
    modes, pattern = probe_modes.shape[1:3]
    margin = pattern // 2
    half = LANES
    devices = lax.axis_size("ty") * lax.axis_size("tx")
    groups = digit_groups()
    f32, bf16 = jnp.float32, jnp.bfloat16
    slots = intensities.shape[2]
    tables = jnp.asarray(fourier_tables(pattern))

    def shape(*sizes):
        return jax.ShapeDtypeStruct(sizes, f32)

    tile, rows_shape = shape(2, length, length), shape(2, margin, length)
    side, tall_side, corner = shape(2, length, margin), shape(2, length + 2 * margin, margin), shape(2, margin, margin)
    core_tile = paired(object_field, "ty", "inner")
    center, chip_rows, inner_side, outer_side = call(
        edges_kernel, "edges", [tile, rows_shape, side, side], (object_field,), "h", scratch=(pltpu.SemaphoreType.DMA((4,)),)
    )
    chip_rows = paired(chip_rows, "ty", "outer")
    inner_side = paired(inner_side, "tx", "inner")
    outer_side = paired(outer_side, "tx", "outer")
    (root,) = call(
        root_kernel,
        "root",
        [shape(slots, 2, half, pattern)],
        (intensities[0, 0],),
        scratch=(pltpu.VMEM((slots, 2, pattern, half), f32),),
        weight=AROUND,
    )
    (scalars,) = call(
        places_kernel, "places", [jax.ShapeDtypeStruct((1 + 2 * slots,), jnp.int32)], (counts.T, offsets[0, 0].T), "ss", "s", weight=AROUND
    )
    inner_corner, outer_corner = call(corners_kernel, "corners", [corner, corner], (chip_rows, root, scalars), "vhh")
    inner_corner = paired(inner_corner, "tx", "inner")
    outer_corner = paired(outer_corner, "tx", "outer")
    inner_near, outer_near = call(near_kernel, "near", [corner, corner], (inner_side, outer_side))
    inner_near = paired(inner_near, "ty", "inner")
    outer_near = paired(outer_near, "ty", "inner")
    (far_rows,) = call(far_kernel, "far", [shape(2, 4, margin, half)], (chip_rows, inner_corner, outer_corner), weight=AHEAD)
    pieces = 1 << sum(len(bits) for _, bits in groups)
    rows = 2 * 2 * modes * pattern // pieces
    kept = shape(pieces // 2, rows, half)
    probe_sent, value, inner_side, outer_side, grad_mid = call(
        slots_kernel,
        "slots",
        [kept, kept, tall_side, tall_side, shape(2, length + 2 * margin, length)],
        (
            scalars, center, core_tile, far_rows, inner_side, outer_side, inner_near, outer_near,
            probe_modes, root, tables,
        ),
        "s",
        scratch=(
            pltpu.VMEM((2, 4, length + 2 * margin, half), f32),
            pltpu.VMEM((2, 4, length + 2 * margin, half), f32),
            pltpu.VMEM((2, 2, pattern, half), f32),
            pltpu.VMEM((modes, 2, pattern, pattern), bf16),
            pltpu.VMEM((modes, 2, pattern, pattern), bf16),
            pltpu.VMEM((modes, 2, pattern, pattern), f32),
            pltpu.VMEM((2 * 2 * modes * pattern, half), f32),
        ),
        limit=VMEM_LIMIT,
    )

    value = added(value, [paired(probe_sent, "ty", "inner")], weight=HEAVY)
    inner_side = paired(inner_side, "tx", "inner")
    outer_side = paired(outer_side, "tx", "outer")
    for group in groups[1:-1]:
        value = added(value, scattered(value, *group))
    value = added(value, scattered(value, *groups[-1]), scale=1.0 / devices)
    core_rows, chip_rows, inner_grad = call(
        rows_kernel,
        "rows",
        [rows_shape, rows_shape, tile],
        (grad_mid, inner_side, outer_side, value),
        "vvvh",
        weight=HEAVY,
    )
    chip_rows = paired(chip_rows, "ty", "outer")
    core_rows = paired(core_rows, "ty", "inner")
    for i in range(1, lax.axis_size("tx").bit_length() - 1):
        value = added(value, [exchanged(value, "tx", 1 << i)])
    for i in range(len(groups) - 1, 0, -1):
        parts = gathered(value, *groups[i])
        joined = shape(len(parts) * value.shape[0], rows, half)
        arrived = chip_rows if i == len(groups) - 1 else core_rows
        (value,) = call(after_kernel, "after", [joined], (arrived, *parts), "h")
    (object_grad,) = call(columns_kernel, "columns", [tile], (inner_grad, core_rows, chip_rows))
    other = paired(value, "ty", "inner")
    sems = (pltpu.SemaphoreType.DMA((pieces // 2,)),)
    (probe_grad,) = call(
        functools.partial(join_kernel, 0), "join", [shape(*probe_modes.shape)], (value,), "v", "h", sems, weight=AROUND
    )
    (probe_grad,) = call(
        functools.partial(join_kernel, pieces // 2),
        "join_rest",
        [shape(*probe_modes.shape)],
        (other, probe_grad),
        "vh",
        "h",
        sems,
        aliases={1: 0},
    )
    return (object_grad, probe_grad)


def solution(mesh):
    placed = (
        P(None, "ty", "tx"),
        P(),
        P("ty", "tx", None, None, None),
        P("ty", "tx", None, None),
        P(),
    )
    return jax.shard_map(
        shards, mesh=mesh, in_specs=placed, out_specs=(P(None, "ty", "tx"), P()), check_vma=False
    )
```

profile of v0, /device:TPU:0, one launch (start us, length us, event | category | flops | bytes accessed | tf_op | source)
XLA Modules:
  0.0 70.6 jit_solution(10624245181034426784)
XLA Ops:
  0.6 0.5 collective-permute-start
  1.1 0.0 copy-start.2
  1.1 1.0 %copy-done.2 = f32[2,256,256]{2,1,0:T(8,128)S(1)} copy-done((f32[2,256,256]{2,1,0:T(8,128)S(1)}, f32[2,256,256]{2,1,0:T(8,128)}, u32[]{:S(2)}) %copy-start.2) | copy-done | bytes 524312
  2.2 0.1 edges.1
  2.3 0.7 collective-permute-start.1
  3.0 2.6 %collective-permute-start.4 = (f32[2,256,128]{2,1,0:T(8,128)S(1)}, f32[2,256,128]{2,1,0:T(8,128)S(1)}, u32[]{:S(2)}, u32[]{:S(2)}) collective-permute-start(f32[2,256,128]{2,1,0:T(8,128)S(1)} %get-tuple-element.22), channel_id=1, source_target_pairs={{0,1},{1,0},{2,3},{3,2},{4,5},{5,4},{6,7},{7,6},{8,9},{9,8},{10,11... | collective-permute-start | bytes 786440 | tf_op jit(solution)/shard_map/ppermute | solution.py:366
  5.7 0.7 collective-permute-start.5
  6.3 0.0 copy-start.3
  6.3 1.1 %copy-done.3 = f32[1,1,3,256,256]{4,3,2,1,0:T(8,128)S(1)} copy-done((f32[1,1,3,256,256]{4,3,2,1,0:T(8,128)S(1)}, f32[1,1,3,256,256]{4,3,2,1,0:T(8,128)}, u32[]{:S(2)}) %copy-start.3) | copy-done | bytes 786456
  7.5 0.0 copy-start.4
  7.5 0.6 root.1._
  8.0 0.1 copy-done.4
  8.2 0.0 copy-done.5
  8.2 1.2 %places.1.__.scalars = s32[7]{0:T(128)S(1)} custom-call(s32[4,8]{1,0:T(4,128)S(1)} %bitcast.6, s32[2,3]{1,0:T(2,128)S(1)} %bitcast.7), custom_call_target="tpu_custom_call" | custom-call | flops 2000000000 | bytes 180 | tf_op jit(solution)/shard_map/places/pallas_call | solution.py:401
  9.4 0.0 collective-permute-done.1.chip_rows
  9.4 4.4 %collective-permute-start.2 = (f32[2,128,128]{2,1,0:T(8,128)S(1)}, f32[2,128,128]{2,1,0:T(8,128)S(1)}, u32[]{:S(2)}, u32[]{:S(2)}) collective-permute-start(f32[2,128,128]{2,1,0:T(8,128)S(1)} %get-tuple-element.20), channel_id=1, source_target_pairs={{0,1},{1,0},{2,3},{3,2},{4,5},{5,4},{6,7},{7,6},{8,9},{9,8},{10,11... | collective-permute-start | bytes 393224 | tf_op jit(solution)/shard_map/ppermute | solution.py:366
  13.9 0.7 collective-permute-start.3
  14.5 0.0 collective-permute-done.4.inner_side
  14.5 0.0 collective-permute-done.5.outer_side
  14.6 2.1 %collective-permute-start.6 = (f32[2,128,128]{2,1,0:T(8,128)S(1)}, f32[2,128,128]{2,1,0:T(8,128)S(1)}, u32[]{:S(2)}, u32[]{:S(2)}) collective-permute-start(f32[2,128,128]{2,1,0:T(8,128)S(1)} %get-tuple-element.24), channel_id=1, source_target_pairs={{0,4},{4,0},{8,12},{12,8},{16,20},{20,16},{24,28},{28,24},{1,5},{5... | collective-permute-start | bytes 393224 | tf_op jit(solution)/shard_map/ppermute | solution.py:366
  16.7 0.1 collective-permute-start.7
  16.8 0.1 collective-permute-done.2.inner_corner
  16.8 0.0 collective-permute-done.3.outer_corner
  16.9 0.8 %collective-permute-done.6.inner_near = f32[2,128,128]{2,1,0:T(8,128)S(1)} collective-permute-done((f32[2,128,128]{2,1,0:T(8,128)S(1)}, f32[2,128,128]{2,1,0:T(8,128)S(1)}, u32[]{:S(2)}, u32[]{:S(2)}) %collective-permute-start.6) | collective-permute-done | bytes 131104 | tf_op jit(solution)/shard_map/ppermute | solution.py:366
  17.6 0.4 collective-permute-done.7.outer_near
  18.0 0.0 collective-permute-done.core_tile
  18.0 0.2 copy-done
  18.2 0.3 copy-done.1
  18.5 6.8 %slots.1 = (f32[8,128,128]{2,1,0:T(8,128)S(1)}, f32[8,128,128]{2,1,0:T(8,128)S(1)}, f32[2,512,128]{2,1,0:T(8,128)S(1)}, f32[2,512,128]{2,1,0:T(8,128)S(1)}, f32[2,512,256]{2,1,0:T(8,128)S(1)}) custom-call(s32[7]{0:T(128)S(1)} %places.1.__.scalars, f32[2,256,256]{2,1,0:T(8,128)S(1)} %get-tuple-element.18.center, ...), custom_call_target="tpu_custom_call" | custom-call | bytes 9437212 | tf_op jit(solution)/shard_map/slots/pallas_call | solution.py:401
  25.3 0.1 collective-permute-start.10
  25.4 1.6 %collective-permute-start.8 = (f32[2,512,128]{2,1,0:T(8,128)S(1)}, f32[2,512,128]{2,1,0:T(8,128)S(1)}, u32[]{:S(2)}, u32[]{:S(2)}) collective-permute-start(f32[2,512,128]{2,1,0:T(8,128)S(1)} %get-tuple-element.27), channel_id=1, source_target_pairs={{0,1},{1,0},{2,3},{3,2},{4,5},{5,4},{6,7},{7,6},{8,9},{9,8},{10,11... | collective-permute-start | bytes 1572872 | tf_op jit(solution)/shard_map/ppermute | solution.py:366
  27.0 0.7 collective-permute-start.9
  27.7 0.0 collective-permute-done.10.refs_0_
  27.7 0.1 add.4.own
  27.8 5.5 %collective-permute-start.13 = (f32[2,128,128]{2,1,0:T(8,128)S(1)}, f32[2,128,128]{2,1,0:T(8,128)S(1)}, u32[]{:S(2)}, u32[]{:S(2)}) collective-permute-start(f32[2,128,128]{2,1,0:T(8,128)S(1)} %get-tuple-element.34), channel_id=1, source_target_pairs={{0,24},{4,28},{8,16},{12,20},{16,8},{20,12},{24,0},{28,4},{1,25},{... | collective-permute-start | bytes 393224 | tf_op jit(solution)/shard_map/ppermute | solution.py:336
  33.3 1.7 %collective-permute-start.12 = (f32[2,128,128]{2,1,0:T(8,128)S(1)}, f32[2,128,128]{2,1,0:T(8,128)S(1)}, u32[]{:S(2)}, u32[]{:S(2)}) collective-permute-start(f32[2,128,128]{2,1,0:T(8,128)S(1)} %get-tuple-element.35), channel_id=1, source_target_pairs={{0,8},{4,12},{8,0},{12,4},{16,24},{20,28},{24,16},{28,20},{1,9},{5... | collective-permute-start | bytes 393224 | tf_op jit(solution)/shard_map/ppermute | solution.py:336
  35.0 0.0 collective-permute-start.11
  35.0 2.4 %collective-permute-done.13.refs_2_ = f32[2,128,128]{2,1,0:T(8,128)S(1)} collective-permute-done((f32[2,128,128]{2,1,0:T(8,128)S(1)}, f32[2,128,128]{2,1,0:T(8,128)S(1)}, u32[]{:S(2)}, u32[]{:S(2)}) %collective-permute-start.13) | collective-permute-done | bytes 131104 | tf_op jit(solution)/shard_map/ppermute | solution.py:336
  37.4 3.9 %collective-permute-done.12.refs_1_ = f32[2,128,128]{2,1,0:T(8,128)S(1)} collective-permute-done((f32[2,128,128]{2,1,0:T(8,128)S(1)}, f32[2,128,128]{2,1,0:T(8,128)S(1)}, u32[]{:S(2)}, u32[]{:S(2)}) %collective-permute-start.12) | collective-permute-done | bytes 131104 | tf_op jit(solution)/shard_map/ppermute | solution.py:336
  41.3 0.0 collective-permute-done.11.refs_0_
  41.4 1.5 %collective-permute-start.14 = (f32[1,128,128]{2,1,0:T(8,128)S(1)}, f32[1,128,128]{2,1,0:T(8,128)S(1)}, u32[]{:S(2)}, u32[]{:S(2)}) collective-permute-start(f32[1,128,128]{2,1,0:T(8,128)S(1)} %slice.19), channel_id=1, source_target_pairs={{0,1},{1,0},{2,3},{3,2},{4,5},{5,4},{6,7},{7,6},{8,9},{9,8},{10,11... | collective-permute-start | bytes 196616 | tf_op jit(solution)/shard_map/ppermute | solution.py:336
  42.9 2.8 %collective-permute-done.14.refs_0_ = f32[1,128,128]{2,1,0:T(8,128)S(1)} collective-permute-done((f32[1,128,128]{2,1,0:T(8,128)S(1)}, f32[1,128,128]{2,1,0:T(8,128)S(1)}, u32[]{:S(2)}, u32[]{:S(2)}) %collective-permute-start.14) | collective-permute-done | bytes 65568 | tf_op jit(solution)/shard_map/ppermute | solution.py:336
  45.7 0.0 collective-permute-done.8.inner_side
  45.7 0.0 collective-permute-done.9.outer_side
  45.8 0.1 rows.1
  45.9 0.7 collective-permute-start.16
  46.6 2.7 %collective-permute-start.17 = (f32[1,128,128]{2,1,0:T(8,128)S(1)}, f32[1,128,128]{2,1,0:T(8,128)S(1)}, u32[]{:S(2)}, u32[]{:S(2)}) collective-permute-start(f32[1,128,128]{2,1,0:T(8,128)S(1)} %add.6._.own), channel_id=1, source_target_pairs={{0,2},{1,3},{2,0},{3,1},{4,6},{5,7},{6,4},{7,5},{8,10},{9,11},{10,... | collective-permute-start | bytes 196616 | tf_op jit(solution)/shard_map/ppermute | solution.py:336
  49.3 3.0 %collective-permute-start.15 = (f32[2,128,256]{2,1,0:T(8,128)S(1)}, f32[2,128,256]{2,1,0:T(8,128)S(1)}, u32[]{:S(2)}, u32[]{:S(2)}) collective-permute-start(f32[2,128,256]{2,1,0:T(8,128)S(1)} %get-tuple-element.32), channel_id=1, source_target_pairs={{0,4},{4,0},{8,12},{12,8},{16,20},{20,16},{24,28},{28,24},{1,5},{5... | collective-permute-start | bytes 786440 | tf_op jit(solution)/shard_map/ppermute | solution.py:366
  52.3 0.0 collective-permute-done.17.refs_0_
  52.4 1.0 %collective-permute-start.18 = (f32[1,128,128]{2,1,0:T(8,128)S(1)}, f32[1,128,128]{2,1,0:T(8,128)S(1)}, u32[]{:S(2)}, u32[]{:S(2)}) collective-permute-start(f32[1,128,128]{2,1,0:T(8,128)S(1)} %add.7.refs_0_), channel_id=1, source_target_pairs={{0,1},{1,0},{2,3},{3,2},{4,5},{5,4},{6,7},{7,6},{8,9},{9,8},{10,11... | collective-permute-start | bytes 196616 | tf_op jit(solution)/shard_map/ppermute | solution.py:336
  53.3 3.4 %collective-permute-done.18.refs_1_ = f32[1,128,128]{2,1,0:T(8,128)S(1)} collective-permute-done((f32[1,128,128]{2,1,0:T(8,128)S(1)}, f32[1,128,128]{2,1,0:T(8,128)S(1)}, u32[]{:S(2)}, u32[]{:S(2)}) %collective-permute-start.18) | collective-permute-done | bytes 65568 | tf_op jit(solution)/shard_map/ppermute | solution.py:336
  56.7 0.0 collective-permute-done.16.chip_in._
  56.8 3.1 %collective-permute-start.21 = (f32[2,128,128]{2,1,0:T(8,128)S(1)}, f32[2,128,128]{2,1,0:T(8,128)S(1)}, u32[]{:S(2)}, u32[]{:S(2)}) collective-permute-start(f32[2,128,128]{2,1,0:T(8,128)S(1)} %after.2.refs_0_), channel_id=1, source_target_pairs={{0,24},{4,28},{8,16},{12,20},{16,8},{20,12},{24,0},{28,4},{1,25},{... | collective-permute-start | bytes 393224 | tf_op jit(solution)/shard_map/ppermute | solution.py:336
  59.8 2.9 %collective-permute-start.20 = (f32[2,128,128]{2,1,0:T(8,128)S(1)}, f32[2,128,128]{2,1,0:T(8,128)S(1)}, u32[]{:S(2)}, u32[]{:S(2)}) collective-permute-start(f32[2,128,128]{2,1,0:T(8,128)S(1)} %after.2.refs_0_), channel_id=1, source_target_pairs={{0,8},{4,12},{8,0},{12,4},{16,24},{20,28},{24,16},{28,20},{1,9},{5... | collective-permute-start | bytes 393224 | tf_op jit(solution)/shard_map/ppermute | solution.py:336
  62.7 0.0 collective-permute-start.19
  62.7 0.0 collective-permute-done.15.core_in._
  62.7 0.9 %collective-permute-done.21.refs_3_ = f32[2,128,128]{2,1,0:T(8,128)S(1)} collective-permute-done((f32[2,128,128]{2,1,0:T(8,128)S(1)}, f32[2,128,128]{2,1,0:T(8,128)S(1)}, u32[]{:S(2)}, u32[]{:S(2)}) %collective-permute-start.21) | collective-permute-done | bytes 131104 | tf_op jit(solution)/shard_map/ppermute | solution.py:336
  63.7 3.9 %collective-permute-done.20.refs_2_ = f32[2,128,128]{2,1,0:T(8,128)S(1)} collective-permute-done((f32[2,128,128]{2,1,0:T(8,128)S(1)}, f32[2,128,128]{2,1,0:T(8,128)S(1)}, u32[]{:S(2)}, u32[]{:S(2)}) %collective-permute-start.20) | collective-permute-done | bytes 131104 | tf_op jit(solution)/shard_map/ppermute | solution.py:336
  67.6 0.1 collective-permute-done.19.refs_1_
  67.7 0.1 collective-permute-start.22
  67.8 0.9 %columns.1 = f32[2,256,256]{2,1,0:T(8,128)} custom-call(f32[2,256,256]{2,1,0:T(8,128)S(1)} %get-tuple-element.31.inner_grad, f32[2,128,256]{2,1,0:T(8,128)S(1)} %collective-permute-done.15.core_in._, f32[2,128,256]{2,1,0:T(8,128)S(1)} %collective-permute-done.16.chip_in._), custom_call_target="tpu_custom_call" | custom-call | bytes 1572864 | tf_op jit(solution)/shard_map/columns/pallas_call | solution.py:401
  68.7 0.8 %join.1.refs_1_ = f32[2,2,256,256]{3,2,1,0:T(8,128)} custom-call(f32[8,128,128]{2,1,0:T(8,128)S(1)} %after.3.refs_0_), custom_call_target="tpu_custom_call" | custom-call | flops 2000000000 | bytes 1572864 | tf_op jit(solution)/shard_map/join/pallas_call | solution.py:401
  69.5 0.2 collective-permute-done.22.refs_0_
  69.7 0.8 %join_rest.1 = f32[2,2,256,256]{3,2,1,0:T(8,128)} custom-call(f32[8,128,128]{2,1,0:T(8,128)S(1)} %collective-permute-done.22.refs_0_, f32[2,2,256,256]{3,2,1,0:T(8,128)} %join.1.refs_1_), custom_call_target="tpu_custom_call", output_to_operand_aliasing={{}: (1, {})} | custom-call | bytes 2621440 | tf_op jit(solution)/shard_map/join_rest/pallas_call | solution.py:401
  (13 shorter events, 0.2 us)
Async XLA Ops:
  0.6 17.4 %collective-permute-start = (f32[2,256,256]{2,1,0:T(8,128)}, f32[2,256,256]{2,1,0:T(8,128)S(1)}, u32[]{:S(2)}, u32[]{:S(2)}) collective-permute-start(f32[2,256,256]{2,1,0:T(8,128)} %field.1), channel_id=1, source_target_pairs={{0,4},{4,0},{8,12},{12,8},{16,20},{20,16},{24,28},{28,24},{1,5},{5... | collective-permute-start | bytes 1572872 | tf_op jit(solution)/shard_map/ppermute | solution.py:366
  1.1 1.0 %copy-start.2 = (f32[2,256,256]{2,1,0:T(8,128)S(1)}, f32[2,256,256]{2,1,0:T(8,128)}, u32[]{:S(2)}) copy-start(f32[2,256,256]{2,1,0:T(8,128)} %field.1) | copy-start | bytes 1572868
  2.3 7.0 %collective-permute-start.1 = (f32[2,128,256]{2,1,0:T(8,128)S(1)}, f32[2,128,256]{2,1,0:T(8,128)S(1)}, u32[]{:S(2)}, u32[]{:S(2)}) collective-permute-start(f32[2,128,256]{2,1,0:T(8,128)S(1)} %get-tuple-element.19), channel_id=1, source_target_pairs={{4,8},{8,4},{12,16},{16,12},{20,24},{24,20},{5,9},{9,5},{13,17},{1... | collective-permute-start | bytes 786440 | tf_op jit(solution)/shard_map/ppermute | solution.py:366
  3.0 11.5 %collective-permute-start.4 = (f32[2,256,128]{2,1,0:T(8,128)S(1)}, f32[2,256,128]{2,1,0:T(8,128)S(1)}, u32[]{:S(2)}, u32[]{:S(2)}) collective-permute-start(f32[2,256,128]{2,1,0:T(8,128)S(1)} %get-tuple-element.22), channel_id=1, source_target_pairs={{0,1},{1,0},{2,3},{3,2},{4,5},{5,4},{6,7},{7,6},{8,9},{9,8},{10,11... | collective-permute-start | bytes 786440 | tf_op jit(solution)/shard_map/ppermute | solution.py:366
  5.7 8.9 %collective-permute-start.5 = (f32[2,256,128]{2,1,0:T(8,128)S(1)}, f32[2,256,128]{2,1,0:T(8,128)S(1)}, u32[]{:S(2)}, u32[]{:S(2)}) collective-permute-start(f32[2,256,128]{2,1,0:T(8,128)S(1)} %get-tuple-element.23), channel_id=1, source_target_pairs={{1,2},{2,1},{5,6},{6,5},{9,10},{10,9},{13,14},{14,13},{17,18},{18,... | collective-permute-start | bytes 786440 | tf_op jit(solution)/shard_map/ppermute | solution.py:366
  6.3 1.1 %copy-start.3 = (f32[1,1,3,256,256]{4,3,2,1,0:T(8,128)S(1)}, f32[1,1,3,256,256]{4,3,2,1,0:T(8,128)}, u32[]{:S(2)}) copy-start(f32[1,1,3,256,256]{4,3,2,1,0:T(8,128)} %param.8) | copy-start | bytes 2359300
  7.5 0.7 copy-start.4
  7.5 0.7 copy-start.5
  9.4 7.4 %collective-permute-start.2 = (f32[2,128,128]{2,1,0:T(8,128)S(1)}, f32[2,128,128]{2,1,0:T(8,128)S(1)}, u32[]{:S(2)}, u32[]{:S(2)}) collective-permute-start(f32[2,128,128]{2,1,0:T(8,128)S(1)} %get-tuple-element.20), channel_id=1, source_target_pairs={{0,1},{1,0},{2,3},{3,2},{4,5},{5,4},{6,7},{7,6},{8,9},{9,8},{10,11... | collective-permute-start | bytes 393224 | tf_op jit(solution)/shard_map/ppermute | solution.py:366
  13.9 3.0 %collective-permute-start.3 = (f32[2,128,128]{2,1,0:T(8,128)S(1)}, f32[2,128,128]{2,1,0:T(8,128)S(1)}, u32[]{:S(2)}, u32[]{:S(2)}) collective-permute-start(f32[2,128,128]{2,1,0:T(8,128)S(1)} %get-tuple-element.21), channel_id=1, source_target_pairs={{1,2},{2,1},{5,6},{6,5},{9,10},{10,9},{13,14},{14,13},{17,18},{18,... | collective-permute-start | bytes 393224 | tf_op jit(solution)/shard_map/ppermute | solution.py:366
  14.6 3.0 %collective-permute-start.6 = (f32[2,128,128]{2,1,0:T(8,128)S(1)}, f32[2,128,128]{2,1,0:T(8,128)S(1)}, u32[]{:S(2)}, u32[]{:S(2)}) collective-permute-start(f32[2,128,128]{2,1,0:T(8,128)S(1)} %get-tuple-element.24), channel_id=1, source_target_pairs={{0,4},{4,0},{8,12},{12,8},{16,20},{20,16},{24,28},{28,24},{1,5},{5... | collective-permute-start | bytes 393224 | tf_op jit(solution)/shard_map/ppermute | solution.py:366
  16.7 1.6 %copy-start = (bf16[8,2,256,256]{3,2,1,0:T(8,128)(2,1)S(1)}, bf16[8,2,256,256]{3,2,1,0:T(8,128)(2,1)}, u32[]{:S(2)}) copy-start(bf16[8,2,256,256]{3,2,1,0:T(8,128)(2,1)} %constant.2.clone.tables) | copy-start | bytes 6291460
  16.7 1.9 %copy-start.1 = (f32[2,2,256,256]{3,2,1,0:T(8,128)S(1)}, f32[2,2,256,256]{3,2,1,0:T(8,128)}, u32[]{:S(2)}) copy-start(f32[2,2,256,256]{3,2,1,0:T(8,128)} %probe.1) | copy-start | bytes 3145732
  16.7 1.3 %collective-permute-start.7 = (f32[2,128,128]{2,1,0:T(8,128)S(1)}, f32[2,128,128]{2,1,0:T(8,128)S(1)}, u32[]{:S(2)}, u32[]{:S(2)}) collective-permute-start(f32[2,128,128]{2,1,0:T(8,128)S(1)} %get-tuple-element.25), channel_id=1, source_target_pairs={{0,4},{4,0},{8,12},{12,8},{16,20},{20,16},{24,28},{28,24},{1,5},{5... | collective-permute-start | bytes 393224 | tf_op jit(solution)/shard_map/ppermute | solution.py:366
  25.3 2.4 %collective-permute-start.10 = (f32[8,128,128]{2,1,0:T(8,128)S(1)}, f32[8,128,128]{2,1,0:T(8,128)S(1)}, u32[]{:S(2)}, u32[]{:S(2)}) collective-permute-start(f32[8,128,128]{2,1,0:T(8,128)S(1)} %get-tuple-element.30), channel_id=1, source_target_pairs={{0,4},{4,0},{8,12},{12,8},{16,20},{20,16},{24,28},{28,24},{1,5},{5... | collective-permute-start | bytes 1572872 | tf_op jit(solution)/shard_map/ppermute | solution.py:366
  25.4 20.4 %collective-permute-start.8 = (f32[2,512,128]{2,1,0:T(8,128)S(1)}, f32[2,512,128]{2,1,0:T(8,128)S(1)}, u32[]{:S(2)}, u32[]{:S(2)}) collective-permute-start(f32[2,512,128]{2,1,0:T(8,128)S(1)} %get-tuple-element.27), channel_id=1, source_target_pairs={{0,1},{1,0},{2,3},{3,2},{4,5},{5,4},{6,7},{7,6},{8,9},{9,8},{10,11... | collective-permute-start | bytes 1572872 | tf_op jit(solution)/shard_map/ppermute | solution.py:366
  27.0 18.8 %collective-permute-start.9 = (f32[2,512,128]{2,1,0:T(8,128)S(1)}, f32[2,512,128]{2,1,0:T(8,128)S(1)}, u32[]{:S(2)}, u32[]{:S(2)}) collective-permute-start(f32[2,512,128]{2,1,0:T(8,128)S(1)} %get-tuple-element.28), channel_id=1, source_target_pairs={{1,2},{2,1},{5,6},{6,5},{9,10},{10,9},{13,14},{14,13},{17,18},{18,... | collective-permute-start | bytes 1572872 | tf_op jit(solution)/shard_map/ppermute | solution.py:366
  27.8 9.6 %collective-permute-start.13 = (f32[2,128,128]{2,1,0:T(8,128)S(1)}, f32[2,128,128]{2,1,0:T(8,128)S(1)}, u32[]{:S(2)}, u32[]{:S(2)}) collective-permute-start(f32[2,128,128]{2,1,0:T(8,128)S(1)} %get-tuple-element.34), channel_id=1, source_target_pairs={{0,24},{4,28},{8,16},{12,20},{16,8},{20,12},{24,0},{28,4},{1,25},{... | collective-permute-start | bytes 393224 | tf_op jit(solution)/shard_map/ppermute | solution.py:336
  33.3 8.1 %collective-permute-start.12 = (f32[2,128,128]{2,1,0:T(8,128)S(1)}, f32[2,128,128]{2,1,0:T(8,128)S(1)}, u32[]{:S(2)}, u32[]{:S(2)}) collective-permute-start(f32[2,128,128]{2,1,0:T(8,128)S(1)} %get-tuple-element.35), channel_id=1, source_target_pairs={{0,8},{4,12},{8,0},{12,4},{16,24},{20,28},{24,16},{28,20},{1,9},{5... | collective-permute-start | bytes 393224 | tf_op jit(solution)/shard_map/ppermute | solution.py:336
  35.0 6.4 %collective-permute-start.11 = (f32[2,128,128]{2,1,0:T(8,128)S(1)}, f32[2,128,128]{2,1,0:T(8,128)S(1)}, u32[]{:S(2)}, u32[]{:S(2)}) collective-permute-start(f32[2,128,128]{2,1,0:T(8,128)S(1)} %get-tuple-element.36), channel_id=1, source_target_pairs={{0,16},{4,20},{8,24},{12,28},{16,0},{20,4},{24,8},{28,12},{1,17},{... | collective-permute-start | bytes 393224 | tf_op jit(solution)/shard_map/ppermute | solution.py:336
  41.4 4.3 %collective-permute-start.14 = (f32[1,128,128]{2,1,0:T(8,128)S(1)}, f32[1,128,128]{2,1,0:T(8,128)S(1)}, u32[]{:S(2)}, u32[]{:S(2)}) collective-permute-start(f32[1,128,128]{2,1,0:T(8,128)S(1)} %slice.19), channel_id=1, source_target_pairs={{0,1},{1,0},{2,3},{3,2},{4,5},{5,4},{6,7},{7,6},{8,9},{9,8},{10,11... | collective-permute-start | bytes 196616 | tf_op jit(solution)/shard_map/ppermute | solution.py:336
  45.9 10.9 %collective-permute-start.16 = (f32[2,128,256]{2,1,0:T(8,128)S(1)}, f32[2,128,256]{2,1,0:T(8,128)S(1)}, u32[]{:S(2)}, u32[]{:S(2)}) collective-permute-start(f32[2,128,256]{2,1,0:T(8,128)S(1)} %get-tuple-element.33), channel_id=1, source_target_pairs={{4,8},{8,4},{12,16},{16,12},{20,24},{24,20},{5,9},{9,5},{13,17},{1... | collective-permute-start | bytes 786440 | tf_op jit(solution)/shard_map/ppermute | solution.py:366
  46.6 5.8 %collective-permute-start.17 = (f32[1,128,128]{2,1,0:T(8,128)S(1)}, f32[1,128,128]{2,1,0:T(8,128)S(1)}, u32[]{:S(2)}, u32[]{:S(2)}) collective-permute-start(f32[1,128,128]{2,1,0:T(8,128)S(1)} %add.6._.own), channel_id=1, source_target_pairs={{0,2},{1,3},{2,0},{3,1},{4,6},{5,7},{6,4},{7,5},{8,10},{9,11},{10,... | collective-permute-start | bytes 196616 | tf_op jit(solution)/shard_map/ppermute | solution.py:336
  49.3 13.4 %collective-permute-start.15 = (f32[2,128,256]{2,1,0:T(8,128)S(1)}, f32[2,128,256]{2,1,0:T(8,128)S(1)}, u32[]{:S(2)}, u32[]{:S(2)}) collective-permute-start(f32[2,128,256]{2,1,0:T(8,128)S(1)} %get-tuple-element.32), channel_id=1, source_target_pairs={{0,4},{4,0},{8,12},{12,8},{16,20},{20,16},{24,28},{28,24},{1,5},{5... | collective-permute-start | bytes 786440 | tf_op jit(solution)/shard_map/ppermute | solution.py:366
  52.4 4.4 %collective-permute-start.18 = (f32[1,128,128]{2,1,0:T(8,128)S(1)}, f32[1,128,128]{2,1,0:T(8,128)S(1)}, u32[]{:S(2)}, u32[]{:S(2)}) collective-permute-start(f32[1,128,128]{2,1,0:T(8,128)S(1)} %add.7.refs_0_), channel_id=1, source_target_pairs={{0,1},{1,0},{2,3},{3,2},{4,5},{5,4},{6,7},{7,6},{8,9},{9,8},{10,11... | collective-permute-start | bytes 196616 | tf_op jit(solution)/shard_map/ppermute | solution.py:336
  56.8 6.9 %collective-permute-start.21 = (f32[2,128,128]{2,1,0:T(8,128)S(1)}, f32[2,128,128]{2,1,0:T(8,128)S(1)}, u32[]{:S(2)}, u32[]{:S(2)}) collective-permute-start(f32[2,128,128]{2,1,0:T(8,128)S(1)} %after.2.refs_0_), channel_id=1, source_target_pairs={{0,24},{4,28},{8,16},{12,20},{16,8},{20,12},{24,0},{28,4},{1,25},{... | collective-permute-start | bytes 393224 | tf_op jit(solution)/shard_map/ppermute | solution.py:336
  59.8 7.8 %collective-permute-start.20 = (f32[2,128,128]{2,1,0:T(8,128)S(1)}, f32[2,128,128]{2,1,0:T(8,128)S(1)}, u32[]{:S(2)}, u32[]{:S(2)}) collective-permute-start(f32[2,128,128]{2,1,0:T(8,128)S(1)} %after.2.refs_0_), channel_id=1, source_target_pairs={{0,8},{4,12},{8,0},{12,4},{16,24},{20,28},{24,16},{28,20},{1,9},{5... | collective-permute-start | bytes 393224 | tf_op jit(solution)/shard_map/ppermute | solution.py:336
  62.7 5.0 %collective-permute-start.19 = (f32[2,128,128]{2,1,0:T(8,128)S(1)}, f32[2,128,128]{2,1,0:T(8,128)S(1)}, u32[]{:S(2)}, u32[]{:S(2)}) collective-permute-start(f32[2,128,128]{2,1,0:T(8,128)S(1)} %after.2.refs_0_), channel_id=1, source_target_pairs={{0,16},{4,20},{8,24},{12,28},{16,0},{20,4},{24,8},{28,12},{1,17},{... | collective-permute-start | bytes 393224 | tf_op jit(solution)/shard_map/ppermute | solution.py:336
  67.7 2.0 %collective-permute-start.22 = (f32[8,128,128]{2,1,0:T(8,128)S(1)}, f32[8,128,128]{2,1,0:T(8,128)S(1)}, u32[]{:S(2)}, u32[]{:S(2)}) collective-permute-start(f32[8,128,128]{2,1,0:T(8,128)S(1)} %after.3.refs_0_), channel_id=1, source_target_pairs={{0,4},{4,0},{8,12},{12,8},{16,20},{20,16},{24,28},{28,24},{1,5},{5... | collective-permute-start | bytes 1572872 | tf_op jit(solution)/shard_map/ppermute | solution.py:366
where the time goes:
time: 72 us; the launch traced here: 70.6 us
  starting transfers between devices  36.3 us (50%)
  waiting for transfers between devices  18.9 us (26%)
  Pallas kernels  11.6 us (16%)
  local copies, waits for them, and re-layouts  2.83 us (4%)
  between operations  0.86 us (1%)
    ppermute x9, starting transfers between devices, exchanged(): lax.ppermute(value, axis, [(i, i ^ mask) for i in range(lax.axis_size(axi...  18.4 us
    ppermute x14, starting transfers between devices, paired(): lax.ppermute(value, axis, [(i, j) for i, j in pairs if 0 <= j < count])  17.9 us
    ppermute x9, waiting for transfers between devices, exchanged(): lax.ppermute(value, axis, [(i, i ^ mask) for i in range(lax.axis_size(axi...  17.5 us
    pallas_call x17, Pallas kernels, call(): pl.pallas_call(body, out_shape=tuple(out), in_specs=specs(spaces, len(ope...  11.6 us
    unnamed x12, local copies, waits for them, and re-layouts  2.8 us
  transfers between devices with their start and end apart: 23, of which 11 were waited for; matrix products, arithmetic and copies ran while one was open for 0% of the time, Pallas kernels for 5%

commit v1 on v0

--- a/solution.py
+++ b/solution.py
@@ -64,11 +64,16 @@
     return pl.multiple_of((1 - odd) * LANES, LANES), pl.multiple_of(odd * LANES, LANES)
 
 
-def edges_kernel(field, center, chip_rows, inner_side, outer_side, sems):
+def chip_edges_kernel(field, chip_rows, sem):
     _, far = near_and_far(LANES)
+    copy = pltpu.make_async_copy(field.at[:, pl.ds(far, LANES), :], chip_rows, sem)
+    copy.start()
+    copy.wait()
+
+
+def edges_kernel(field, _, center, inner_side, outer_side, sems):
     inner, outer = inner_and_outer()
     moves = (
-        (field.at[:, pl.ds(far, LANES), :], chip_rows),
         (field.at[:, :, pl.ds(inner, LANES)], inner_side),
         (field.at[:, :, pl.ds(outer, LANES)], outer_side),
         (field, center),
@@ -428,9 +433,11 @@
     tile, rows_shape = shape(2, length, length), shape(2, margin, length)
     side, tall_side, corner = shape(2, length, margin), shape(2, length + 2 * margin, margin), shape(2, margin, margin)
     core_tile = paired(object_field, "ty", "inner")
-    center, chip_rows, inner_side, outer_side = call(
-        edges_kernel, "edges", [tile, rows_shape, side, side], (object_field,), "h", scratch=(pltpu.SemaphoreType.DMA((4,)),)
-    )
+    (leaving,) = call(chip_edges_kernel, "chip_edges", [rows_shape], (object_field,), "h", scratch=(pltpu.SemaphoreType.DMA,))
+    center, inner_side, outer_side = call(
+        edges_kernel, "edges", [tile, side, side], (object_field, leaving), "hh", scratch=(pltpu.SemaphoreType.DMA((3,)),), weight=AROUND
+    )
+    chip_rows = leaving
     chip_rows = paired(chip_rows, "ty", "outer")
     inner_side = paired(inner_side, "tx", "inner")
     outer_side = paired(outer_side, "tx", "outer")
@@ -493,12 +500,12 @@
     chip_rows = paired(chip_rows, "ty", "outer")
     core_rows = paired(core_rows, "ty", "inner")
     for i in range(1, lax.axis_size("tx").bit_length() - 1):
-        value = added(value, [exchanged(value, "tx", 1 << i)])
+        value = added(value, [exchanged(value, "tx", 1 << i)], weight=4000000000)
     for i in range(len(groups) - 1, 0, -1):
         parts = gathered(value, *groups[i])
         joined = shape(len(parts) * value.shape[0], rows, half)
         arrived = chip_rows if i == len(groups) - 1 else core_rows
-        (value,) = call(after_kernel, "after", [joined], (arrived, *parts), "h")
+        (value,) = call(after_kernel, "after", [joined], (arrived, *parts), "h", weight=4000000000)
     (object_grad,) = call(columns_kernel, "columns", [tile], (inner_grad, core_rows, chip_rows))
     other = paired(value, "ty", "inner")
     sems = (pltpu.SemaphoreType.DMA((pieces // 2,)),)

time: 72 us -> 70.3 us (0.976); the launches traced: 70.6 us -> 70.3 us
  starting transfers between devices: 36.3 us -> 39.4 us
  Pallas kernels: 11.6 us -> 8.78 us
  local copies, waits for them, and re-layouts: 2.83 us -> 1.7 us
    ppermute x14, starting transfers between devices: 17.9 us -> 21.3 us  [paired(): lax.ppermute(value, axis, [(i, j) for i, j in pairs if 0 <= j < count])]
    pallas_call x17 -> x18, Pallas kernels: 11.6 us -> 8.78 us  [call(): pl.pallas_call(body, out_shape=tuple(out), in_specs=specs(spaces, len(ope...]
    unnamed x12, local copies, waits for them, and re-layouts: 2.8 us -> 1.67 us
  transfers between devices with their start and end apart: 23 -> 23, of which waited for: 11 -> 12; matrix products, arithmetic and copies ran while one was open for 0% -> 0% of each run, Pallas kernels for 5% -> 6%
where the time goes in v1:
time: 70.3 us
  starting transfers between devices  39.4 us (56%)
  waiting for transfers between devices  19.5 us (28%)
  Pallas kernels  8.78 us (12%)
  local copies, waits for them, and re-layouts  1.7 us (2%)
  between operations  0.88 us (1%)
    ppermute x14, starting transfers between devices, paired(): lax.ppermute(value, axis, [(i, j) for i, j in pairs if 0 <= j < count])  21.3 us
    ppermute x9, starting transfers between devices, exchanged(): lax.ppermute(value, axis, [(i, i ^ mask) for i in range(lax.axis_size(axi...  18.1 us
    ppermute x9, waiting for transfers between devices, exchanged(): lax.ppermute(value, axis, [(i, i ^ mask) for i in range(lax.axis_size(axi...  18.1 us
    pallas_call x18, Pallas kernels, call(): pl.pallas_call(body, out_shape=tuple(out), in_specs=specs(spaces, len(ope...  8.78 us
    unnamed x12, local copies, waits for them, and re-layouts  1.67 us
    ppermute x14, waiting for transfers between devices, paired(): lax.ppermute(value, axis, [(i, j) for i, j in pairs if 0 <= j < count])  1.41 us
  transfers between devices with their start and end apart: 23, of which 12 were waited for; matrix products, arithmetic and copies ran while one was open for 0% of the time, Pallas kernels for 6%

profile of v1, /device:TPU:0, one launch (start us, length us, event | category | flops | bytes accessed | tf_op | source)
XLA Modules:
  0.0 70.3 jit_solution(16111345996207718896)
XLA Ops:
  0.6 0.5 collective-permute-start
  1.1 1.0 %copy-done.2 = f32[2,256,256]{2,1,0:T(8,128)S(1)} copy-done((f32[2,256,256]{2,1,0:T(8,128)S(1)}, f32[2,256,256]{2,1,0:T(8,128)}, u32[]{:S(2)}) %copy-start.2) | copy-done | bytes 524312
  2.2 0.0 copy-start.3
  2.2 0.8 %collective-permute-start.1 = (f32[2,128,256]{2,1,0:T(8,128)S(1)}, f32[2,128,256]{2,1,0:T(8,128)S(1)}, u32[]{:S(2)}, u32[]{:S(2)}) collective-permute-start(f32[2,128,256]{2,1,0:T(8,128)S(1)} %chip_edges.1._), channel_id=1, source_target_pairs={{4,8},{8,4},{12,16},{16,12},{20,24},{24,20},{5,9},{9,5},{13,17},{1... | collective-permute-start | bytes 786440 | tf_op jit(solution)/shard_map/ppermute | solution.py:371
  3.1 0.1 edges.1
  3.2 2.6 %collective-permute-start.4 = (f32[2,256,128]{2,1,0:T(8,128)S(1)}, f32[2,256,128]{2,1,0:T(8,128)S(1)}, u32[]{:S(2)}, u32[]{:S(2)}) collective-permute-start(f32[2,256,128]{2,1,0:T(8,128)S(1)} %get-tuple-element.20), channel_id=1, source_target_pairs={{0,1},{1,0},{2,3},{3,2},{4,5},{5,4},{6,7},{7,6},{8,9},{9,8},{10,11... | collective-permute-start | bytes 786440 | tf_op jit(solution)/shard_map/ppermute | solution.py:371
  5.8 0.7 collective-permute-start.5
  6.5 0.0 copy-done.3
  6.5 0.0 copy-start.4
  6.5 0.0 copy-start.5
  6.5 0.6 root.1._
  7.1 0.1 copy-done.4
  7.2 0.0 copy-done.5
  7.2 1.2 %places.1.__.scalars = s32[7]{0:T(128)S(1)} custom-call(s32[4,8]{1,0:T(4,128)S(1)} %bitcast.6, s32[2,3]{1,0:T(2,128)S(1)} %bitcast.7), custom_call_target="tpu_custom_call" | custom-call | flops 2000000000 | bytes 180 | tf_op jit(solution)/shard_map/places/pallas_call | solution.py:406
  8.4 0.0 collective-permute-done.1.chip_rows
  8.5 4.4 %collective-permute-start.2 = (f32[2,128,128]{2,1,0:T(8,128)S(1)}, f32[2,128,128]{2,1,0:T(8,128)S(1)}, u32[]{:S(2)}, u32[]{:S(2)}) collective-permute-start(f32[2,128,128]{2,1,0:T(8,128)S(1)} %get-tuple-element.18), channel_id=1, source_target_pairs={{0,1},{1,0},{2,3},{3,2},{4,5},{5,4},{6,7},{7,6},{8,9},{9,8},{10,11... | collective-permute-start | bytes 393224 | tf_op jit(solution)/shard_map/ppermute | solution.py:371
  12.9 0.7 collective-permute-start.3
  13.6 0.0 collective-permute-done.4.inner_side
  13.6 0.0 collective-permute-done.5.outer_side
  13.6 2.9 %collective-permute-start.6 = (f32[2,128,128]{2,1,0:T(8,128)S(1)}, f32[2,128,128]{2,1,0:T(8,128)S(1)}, u32[]{:S(2)}, u32[]{:S(2)}) collective-permute-start(f32[2,128,128]{2,1,0:T(8,128)S(1)} %get-tuple-element.22), channel_id=1, source_target_pairs={{0,4},{4,0},{8,12},{12,8},{16,20},{20,16},{24,28},{28,24},{1,5},{5... | collective-permute-start | bytes 393224 | tf_op jit(solution)/shard_map/ppermute | solution.py:371
  16.6 0.1 collective-permute-start.7
  16.7 0.0 collective-permute-done.2.inner_corner
  16.7 0.0 collective-permute-done.3.outer_corner
  16.7 0.8 %collective-permute-done.6.inner_near = f32[2,128,128]{2,1,0:T(8,128)S(1)} collective-permute-done((f32[2,128,128]{2,1,0:T(8,128)S(1)}, f32[2,128,128]{2,1,0:T(8,128)S(1)}, u32[]{:S(2)}, u32[]{:S(2)}) %collective-permute-start.6) | collective-permute-done | bytes 131104 | tf_op jit(solution)/shard_map/ppermute | solution.py:371
  17.5 0.4 collective-permute-done.7.outer_near
  17.9 0.0 collective-permute-done.core_tile
  17.9 0.2 copy-done
  18.2 0.3 copy-done.1
  18.4 4.0 %slots.1 = (f32[8,128,128]{2,1,0:T(8,128)S(1)}, f32[8,128,128]{2,1,0:T(8,128)S(1)}, f32[2,512,128]{2,1,0:T(8,128)S(1)}, f32[2,512,128]{2,1,0:T(8,128)S(1)}, f32[2,512,256]{2,1,0:T(8,128)S(1)}) custom-call(s32[7]{0:T(128)S(1)} %places.1.__.scalars, f32[2,256,256]{2,1,0:T(8,128)S(1)} %get-tuple-element.17.center, ...), custom_call_target="tpu_custom_call" | custom-call | bytes 9437212 | tf_op jit(solution)/shard_map/slots/pallas_call | solution.py:406
  22.4 2.9 %collective-permute-start.10 = (f32[8,128,128]{2,1,0:T(8,128)S(1)}, f32[8,128,128]{2,1,0:T(8,128)S(1)}, u32[]{:S(2)}, u32[]{:S(2)}) collective-permute-start(f32[8,128,128]{2,1,0:T(8,128)S(1)} %get-tuple-element.28), channel_id=1, source_target_pairs={{0,4},{4,0},{8,12},{12,8},{16,20},{20,16},{24,28},{28,24},{1,5},{5... | collective-permute-start | bytes 1572872 | tf_op jit(solution)/shard_map/ppermute | solution.py:371
  25.3 4.2 %collective-permute-start.8 = (f32[2,512,128]{2,1,0:T(8,128)S(1)}, f32[2,512,128]{2,1,0:T(8,128)S(1)}, u32[]{:S(2)}, u32[]{:S(2)}) collective-permute-start(f32[2,512,128]{2,1,0:T(8,128)S(1)} %get-tuple-element.25), channel_id=1, source_target_pairs={{0,1},{1,0},{2,3},{3,2},{4,5},{5,4},{6,7},{7,6},{8,9},{9,8},{10,11... | collective-permute-start | bytes 1572872 | tf_op jit(solution)/shard_map/ppermute | solution.py:371
  29.4 0.7 collective-permute-start.9
  30.1 0.0 collective-permute-done.10.refs_0_
  30.1 0.1 add.4.own
  30.2 5.3 %collective-permute-start.13 = (f32[2,128,128]{2,1,0:T(8,128)S(1)}, f32[2,128,128]{2,1,0:T(8,128)S(1)}, u32[]{:S(2)}, u32[]{:S(2)}) collective-permute-start(f32[2,128,128]{2,1,0:T(8,128)S(1)} %get-tuple-element.32), channel_id=1, source_target_pairs={{0,24},{4,28},{8,16},{12,20},{16,8},{20,12},{24,0},{28,4},{1,25},{... | collective-permute-start | bytes 393224 | tf_op jit(solution)/shard_map/ppermute | solution.py:341
  35.5 0.0 collective-permute-start.12
  35.5 0.6 collective-permute-start.11
  36.1 3.7 %collective-permute-done.13.refs_2_ = f32[2,128,128]{2,1,0:T(8,128)S(1)} collective-permute-done((f32[2,128,128]{2,1,0:T(8,128)S(1)}, f32[2,128,128]{2,1,0:T(8,128)S(1)}, u32[]{:S(2)}, u32[]{:S(2)}) %collective-permute-start.13) | collective-permute-done | bytes 131104 | tf_op jit(solution)/shard_map/ppermute | solution.py:341
  39.8 1.2 %collective-permute-done.12.refs_1_ = f32[2,128,128]{2,1,0:T(8,128)S(1)} collective-permute-done((f32[2,128,128]{2,1,0:T(8,128)S(1)}, f32[2,128,128]{2,1,0:T(8,128)S(1)}, u32[]{:S(2)}, u32[]{:S(2)}) %collective-permute-start.12) | collective-permute-done | bytes 131104 | tf_op jit(solution)/shard_map/ppermute | solution.py:341
  41.0 0.7 %collective-permute-done.11.refs_0_ = f32[2,128,128]{2,1,0:T(8,128)S(1)} collective-permute-done((f32[2,128,128]{2,1,0:T(8,128)S(1)}, f32[2,128,128]{2,1,0:T(8,128)S(1)}, u32[]{:S(2)}, u32[]{:S(2)}) %collective-permute-start.11) | collective-permute-done | bytes 131104 | tf_op jit(solution)/shard_map/ppermute | solution.py:341
  41.8 1.6 %collective-permute-start.14 = (f32[1,128,128]{2,1,0:T(8,128)S(1)}, f32[1,128,128]{2,1,0:T(8,128)S(1)}, u32[]{:S(2)}, u32[]{:S(2)}) collective-permute-start(f32[1,128,128]{2,1,0:T(8,128)S(1)} %slice.19), channel_id=1, source_target_pairs={{0,1},{1,0},{2,3},{3,2},{4,5},{5,4},{6,7},{7,6},{8,9},{9,8},{10,11... | collective-permute-start | bytes 196616 | tf_op jit(solution)/shard_map/ppermute | solution.py:341
  43.4 2.7 %collective-permute-done.14.refs_0_ = f32[1,128,128]{2,1,0:T(8,128)S(1)} collective-permute-done((f32[1,128,128]{2,1,0:T(8,128)S(1)}, f32[1,128,128]{2,1,0:T(8,128)S(1)}, u32[]{:S(2)}, u32[]{:S(2)}) %collective-permute-start.14) | collective-permute-done | bytes 65568 | tf_op jit(solution)/shard_map/ppermute | solution.py:341
  46.2 2.8 %collective-permute-start.17 = (f32[1,128,128]{2,1,0:T(8,128)S(1)}, f32[1,128,128]{2,1,0:T(8,128)S(1)}, u32[]{:S(2)}, u32[]{:S(2)}) collective-permute-start(f32[1,128,128]{2,1,0:T(8,128)S(1)} %add.6._.own), channel_id=1, source_target_pairs={{0,2},{1,3},{2,0},{3,1},{4,6},{5,7},{6,4},{7,5},{8,10},{9,11},{10,... | collective-permute-start | bytes 196616 | tf_op jit(solution)/shard_map/ppermute | solution.py:341
  48.9 0.0 collective-permute-done.8.inner_side
  48.9 0.0 collective-permute-done.9.outer_side
  48.9 0.1 rows.1
  49.1 0.7 collective-permute-start.16
  49.8 1.6 %collective-permute-done.17.refs_0_ = f32[1,128,128]{2,1,0:T(8,128)S(1)} collective-permute-done((f32[1,128,128]{2,1,0:T(8,128)S(1)}, f32[1,128,128]{2,1,0:T(8,128)S(1)}, u32[]{:S(2)}, u32[]{:S(2)}) %collective-permute-start.17) | collective-permute-done | bytes 65568 | tf_op jit(solution)/shard_map/ppermute | solution.py:341
  51.4 1.6 %collective-permute-start.18 = (f32[1,128,128]{2,1,0:T(8,128)S(1)}, f32[1,128,128]{2,1,0:T(8,128)S(1)}, u32[]{:S(2)}, u32[]{:S(2)}) collective-permute-start(f32[1,128,128]{2,1,0:T(8,128)S(1)} %add.7.refs_0_), channel_id=1, source_target_pairs={{0,1},{1,0},{2,3},{3,2},{4,5},{5,4},{6,7},{7,6},{8,9},{9,8},{10,11... | collective-permute-start | bytes 196616 | tf_op jit(solution)/shard_map/ppermute | solution.py:341
  53.0 0.0 collective-permute-start.15
  53.0 3.0 %collective-permute-done.18.refs_1_ = f32[1,128,128]{2,1,0:T(8,128)S(1)} collective-permute-done((f32[1,128,128]{2,1,0:T(8,128)S(1)}, f32[1,128,128]{2,1,0:T(8,128)S(1)}, u32[]{:S(2)}, u32[]{:S(2)}) %collective-permute-start.18) | collective-permute-done | bytes 65568 | tf_op jit(solution)/shard_map/ppermute | solution.py:341
  56.0 0.0 collective-permute-done.16.chip_in._
  56.0 4.2 %collective-permute-start.21 = (f32[2,128,128]{2,1,0:T(8,128)S(1)}, f32[2,128,128]{2,1,0:T(8,128)S(1)}, u32[]{:S(2)}, u32[]{:S(2)}) collective-permute-start(f32[2,128,128]{2,1,0:T(8,128)S(1)} %after.2.refs_0_), channel_id=1, source_target_pairs={{0,24},{4,28},{8,16},{12,20},{16,8},{20,12},{24,0},{28,4},{1,25},{... | collective-permute-start | bytes 393224 | tf_op jit(solution)/shard_map/ppermute | solution.py:341
  60.2 2.0 %collective-permute-start.20 = (f32[2,128,128]{2,1,0:T(8,128)S(1)}, f32[2,128,128]{2,1,0:T(8,128)S(1)}, u32[]{:S(2)}, u32[]{:S(2)}) collective-permute-start(f32[2,128,128]{2,1,0:T(8,128)S(1)} %after.2.refs_0_), channel_id=1, source_target_pairs={{0,8},{4,12},{8,0},{12,4},{16,24},{20,28},{24,16},{28,20},{1,9},{5... | collective-permute-start | bytes 393224 | tf_op jit(solution)/shard_map/ppermute | solution.py:341
  62.3 0.0 collective-permute-start.19
  62.3 0.0 collective-permute-done.15.core_in._
  62.3 1.8 %collective-permute-done.21.refs_3_ = f32[2,128,128]{2,1,0:T(8,128)S(1)} collective-permute-done((f32[2,128,128]{2,1,0:T(8,128)S(1)}, f32[2,128,128]{2,1,0:T(8,128)S(1)}, u32[]{:S(2)}, u32[]{:S(2)}) %collective-permute-start.21) | collective-permute-done | bytes 131104 | tf_op jit(solution)/shard_map/ppermute | solution.py:341
  64.1 2.6 %collective-permute-done.20.refs_2_ = f32[2,128,128]{2,1,0:T(8,128)S(1)} collective-permute-done((f32[2,128,128]{2,1,0:T(8,128)S(1)}, f32[2,128,128]{2,1,0:T(8,128)S(1)}, u32[]{:S(2)}, u32[]{:S(2)}) %collective-permute-start.20) | collective-permute-done | bytes 131104 | tf_op jit(solution)/shard_map/ppermute | solution.py:341
  66.7 0.7 %collective-permute-done.19.refs_1_ = f32[2,128,128]{2,1,0:T(8,128)S(1)} collective-permute-done((f32[2,128,128]{2,1,0:T(8,128)S(1)}, f32[2,128,128]{2,1,0:T(8,128)S(1)}, u32[]{:S(2)}, u32[]{:S(2)}) %collective-permute-start.19) | collective-permute-done | bytes 131104 | tf_op jit(solution)/shard_map/ppermute | solution.py:341
  67.4 0.1 collective-permute-start.22
  67.5 0.9 %columns.1 = f32[2,256,256]{2,1,0:T(8,128)} custom-call(f32[2,256,256]{2,1,0:T(8,128)S(1)} %get-tuple-element.29.inner_grad, f32[2,128,256]{2,1,0:T(8,128)S(1)} %collective-permute-done.15.core_in._, f32[2,128,256]{2,1,0:T(8,128)S(1)} %collective-permute-done.16.chip_in._), custom_call_target="tpu_custom_call" | custom-call | bytes 1572864 | tf_op jit(solution)/shard_map/columns/pallas_call | solution.py:406
  68.4 0.8 %join.1.refs_1_ = f32[2,2,256,256]{3,2,1,0:T(8,128)} custom-call(f32[8,128,128]{2,1,0:T(8,128)S(1)} %after.3.refs_0_), custom_call_target="tpu_custom_call" | custom-call | flops 2000000000 | bytes 1572864 | tf_op jit(solution)/shard_map/join/pallas_call | solution.py:406
  69.2 0.2 collective-permute-done.22.refs_0_
  69.4 0.8 %join_rest.1 = f32[2,2,256,256]{3,2,1,0:T(8,128)} custom-call(f32[8,128,128]{2,1,0:T(8,128)S(1)} %collective-permute-done.22.refs_0_, f32[2,2,256,256]{3,2,1,0:T(8,128)} %join.1.refs_1_), custom_call_target="tpu_custom_call", output_to_operand_aliasing={{}: (1, {})} | custom-call | bytes 2621440 | tf_op jit(solution)/shard_map/join_rest/pallas_call | solution.py:406
  (14 shorter events, 0.3 us)
Async XLA Ops:
  0.6 17.3 %collective-permute-start = (f32[2,256,256]{2,1,0:T(8,128)}, f32[2,256,256]{2,1,0:T(8,128)S(1)}, u32[]{:S(2)}, u32[]{:S(2)}) collective-permute-start(f32[2,256,256]{2,1,0:T(8,128)} %field.3), channel_id=1, source_target_pairs={{0,4},{4,0},{8,12},{12,8},{16,20},{20,16},{24,28},{28,24},{1,5},{5... | collective-permute-start | bytes 1572872 | tf_op jit(solution)/shard_map/ppermute | solution.py:371
  1.1 1.0 %copy-start.2 = (f32[2,256,256]{2,1,0:T(8,128)S(1)}, f32[2,256,256]{2,1,0:T(8,128)}, u32[]{:S(2)}) copy-start(f32[2,256,256]{2,1,0:T(8,128)} %field.3) | copy-start | bytes 1572868
  2.2 4.3 %copy-start.3 = (f32[1,1,3,256,256]{4,3,2,1,0:T(8,128)S(1)}, f32[1,1,3,256,256]{4,3,2,1,0:T(8,128)}, u32[]{:S(2)}) copy-start(f32[1,1,3,256,256]{4,3,2,1,0:T(8,128)} %param.8) | copy-start | bytes 2359300
  2.2 6.2 %collective-permute-start.1 = (f32[2,128,256]{2,1,0:T(8,128)S(1)}, f32[2,128,256]{2,1,0:T(8,128)S(1)}, u32[]{:S(2)}, u32[]{:S(2)}) collective-permute-start(f32[2,128,256]{2,1,0:T(8,128)S(1)} %chip_edges.1._), channel_id=1, source_target_pairs={{4,8},{8,4},{12,16},{16,12},{20,24},{24,20},{5,9},{9,5},{13,17},{1... | collective-permute-start | bytes 786440 | tf_op jit(solution)/shard_map/ppermute | solution.py:371
  3.2 10.4 %collective-permute-start.4 = (f32[2,256,128]{2,1,0:T(8,128)S(1)}, f32[2,256,128]{2,1,0:T(8,128)S(1)}, u32[]{:S(2)}, u32[]{:S(2)}) collective-permute-start(f32[2,256,128]{2,1,0:T(8,128)S(1)} %get-tuple-element.20), channel_id=1, source_target_pairs={{0,1},{1,0},{2,3},{3,2},{4,5},{5,4},{6,7},{7,6},{8,9},{9,8},{10,11... | collective-permute-start | bytes 786440 | tf_op jit(solution)/shard_map/ppermute | solution.py:371
  5.8 7.8 %collective-permute-start.5 = (f32[2,256,128]{2,1,0:T(8,128)S(1)}, f32[2,256,128]{2,1,0:T(8,128)S(1)}, u32[]{:S(2)}, u32[]{:S(2)}) collective-permute-start(f32[2,256,128]{2,1,0:T(8,128)S(1)} %get-tuple-element.21), channel_id=1, source_target_pairs={{1,2},{2,1},{5,6},{6,5},{9,10},{10,9},{13,14},{14,13},{17,18},{18,... | collective-permute-start | bytes 786440 | tf_op jit(solution)/shard_map/ppermute | solution.py:371
  6.5 0.7 copy-start.4
  6.5 0.7 copy-start.5
  8.5 8.2 %collective-permute-start.2 = (f32[2,128,128]{2,1,0:T(8,128)S(1)}, f32[2,128,128]{2,1,0:T(8,128)S(1)}, u32[]{:S(2)}, u32[]{:S(2)}) collective-permute-start(f32[2,128,128]{2,1,0:T(8,128)S(1)} %get-tuple-element.18), channel_id=1, source_target_pairs={{0,1},{1,0},{2,3},{3,2},{4,5},{5,4},{6,7},{7,6},{8,9},{9,8},{10,11... | collective-permute-start | bytes 393224 | tf_op jit(solution)/shard_map/ppermute | solution.py:371
  12.9 3.8 %collective-permute-start.3 = (f32[2,128,128]{2,1,0:T(8,128)S(1)}, f32[2,128,128]{2,1,0:T(8,128)S(1)}, u32[]{:S(2)}, u32[]{:S(2)}) collective-permute-start(f32[2,128,128]{2,1,0:T(8,128)S(1)} %get-tuple-element.19), channel_id=1, source_target_pairs={{1,2},{2,1},{5,6},{6,5},{9,10},{10,9},{13,14},{14,13},{17,18},{18,... | collective-permute-start | bytes 393224 | tf_op jit(solution)/shard_map/ppermute | solution.py:371
  13.6 3.9 %collective-permute-start.6 = (f32[2,128,128]{2,1,0:T(8,128)S(1)}, f32[2,128,128]{2,1,0:T(8,128)S(1)}, u32[]{:S(2)}, u32[]{:S(2)}) collective-permute-start(f32[2,128,128]{2,1,0:T(8,128)S(1)} %get-tuple-element.22), channel_id=1, source_target_pairs={{0,4},{4,0},{8,12},{12,8},{16,20},{20,16},{24,28},{28,24},{1,5},{5... | collective-permute-start | bytes 393224 | tf_op jit(solution)/shard_map/ppermute | solution.py:371
  16.6 1.6 %copy-start = (bf16[8,2,256,256]{3,2,1,0:T(8,128)(2,1)S(1)}, bf16[8,2,256,256]{3,2,1,0:T(8,128)(2,1)}, u32[]{:S(2)}) copy-start(bf16[8,2,256,256]{3,2,1,0:T(8,128)(2,1)} %constant.2.clone.tables) | copy-start | bytes 6291460
  16.6 1.9 %copy-start.1 = (f32[2,2,256,256]{3,2,1,0:T(8,128)S(1)}, f32[2,2,256,256]{3,2,1,0:T(8,128)}, u32[]{:S(2)}) copy-start(f32[2,2,256,256]{3,2,1,0:T(8,128)} %probe.1) | copy-start | bytes 3145732
  16.6 1.3 %collective-permute-start.7 = (f32[2,128,128]{2,1,0:T(8,128)S(1)}, f32[2,128,128]{2,1,0:T(8,128)S(1)}, u32[]{:S(2)}, u32[]{:S(2)}) collective-permute-start(f32[2,128,128]{2,1,0:T(8,128)S(1)} %get-tuple-element.23), channel_id=1, source_target_pairs={{0,4},{4,0},{8,12},{12,8},{16,20},{20,16},{24,28},{28,24},{1,5},{5... | collective-permute-start | bytes 393224 | tf_op jit(solution)/shard_map/ppermute | solution.py:371
  22.4 7.8 %collective-permute-start.10 = (f32[8,128,128]{2,1,0:T(8,128)S(1)}, f32[8,128,128]{2,1,0:T(8,128)S(1)}, u32[]{:S(2)}, u32[]{:S(2)}) collective-permute-start(f32[8,128,128]{2,1,0:T(8,128)S(1)} %get-tuple-element.28), channel_id=1, source_target_pairs={{0,4},{4,0},{8,12},{12,8},{16,20},{20,16},{24,28},{28,24},{1,5},{5... | collective-permute-start | bytes 1572872 | tf_op jit(solution)/shard_map/ppermute | solution.py:371
  25.3 23.6 %collective-permute-start.8 = (f32[2,512,128]{2,1,0:T(8,128)S(1)}, f32[2,512,128]{2,1,0:T(8,128)S(1)}, u32[]{:S(2)}, u32[]{:S(2)}) collective-permute-start(f32[2,512,128]{2,1,0:T(8,128)S(1)} %get-tuple-element.25), channel_id=1, source_target_pairs={{0,1},{1,0},{2,3},{3,2},{4,5},{5,4},{6,7},{7,6},{8,9},{9,8},{10,11... | collective-permute-start | bytes 1572872 | tf_op jit(solution)/shard_map/ppermute | solution.py:371
  29.4 19.5 %collective-permute-start.9 = (f32[2,512,128]{2,1,0:T(8,128)S(1)}, f32[2,512,128]{2,1,0:T(8,128)S(1)}, u32[]{:S(2)}, u32[]{:S(2)}) collective-permute-start(f32[2,512,128]{2,1,0:T(8,128)S(1)} %get-tuple-element.26), channel_id=1, source_target_pairs={{1,2},{2,1},{5,6},{6,5},{9,10},{10,9},{13,14},{14,13},{17,18},{18,... | collective-permute-start | bytes 1572872 | tf_op jit(solution)/shard_map/ppermute | solution.py:371
  30.2 9.6 %collective-permute-start.13 = (f32[2,128,128]{2,1,0:T(8,128)S(1)}, f32[2,128,128]{2,1,0:T(8,128)S(1)}, u32[]{:S(2)}, u32[]{:S(2)}) collective-permute-start(f32[2,128,128]{2,1,0:T(8,128)S(1)} %get-tuple-element.32), channel_id=1, source_target_pairs={{0,24},{4,28},{8,16},{12,20},{16,8},{20,12},{24,0},{28,4},{1,25},{... | collective-permute-start | bytes 393224 | tf_op jit(solution)/shard_map/ppermute | solution.py:341
  35.5 5.5 %collective-permute-start.12 = (f32[2,128,128]{2,1,0:T(8,128)S(1)}, f32[2,128,128]{2,1,0:T(8,128)S(1)}, u32[]{:S(2)}, u32[]{:S(2)}) collective-permute-start(f32[2,128,128]{2,1,0:T(8,128)S(1)} %get-tuple-element.33), channel_id=1, source_target_pairs={{0,8},{4,12},{8,0},{12,4},{16,24},{20,28},{24,16},{28,20},{1,9},{5... | collective-permute-start | bytes 393224 | tf_op jit(solution)/shard_map/ppermute | solution.py:341
  35.5 6.3 %collective-permute-start.11 = (f32[2,128,128]{2,1,0:T(8,128)S(1)}, f32[2,128,128]{2,1,0:T(8,128)S(1)}, u32[]{:S(2)}, u32[]{:S(2)}) collective-permute-start(f32[2,128,128]{2,1,0:T(8,128)S(1)} %get-tuple-element.34), channel_id=1, source_target_pairs={{0,16},{4,20},{8,24},{12,28},{16,0},{20,4},{24,8},{28,12},{1,17},{... | collective-permute-start | bytes 393224 | tf_op jit(solution)/shard_map/ppermute | solution.py:341
  41.8 4.3 %collective-permute-start.14 = (f32[1,128,128]{2,1,0:T(8,128)S(1)}, f32[1,128,128]{2,1,0:T(8,128)S(1)}, u32[]{:S(2)}, u32[]{:S(2)}) collective-permute-start(f32[1,128,128]{2,1,0:T(8,128)S(1)} %slice.19), channel_id=1, source_target_pairs={{0,1},{1,0},{2,3},{3,2},{4,5},{5,4},{6,7},{7,6},{8,9},{9,8},{10,11... | collective-permute-start | bytes 196616 | tf_op jit(solution)/shard_map/ppermute | solution.py:341
  46.2 5.2 %collective-permute-start.17 = (f32[1,128,128]{2,1,0:T(8,128)S(1)}, f32[1,128,128]{2,1,0:T(8,128)S(1)}, u32[]{:S(2)}, u32[]{:S(2)}) collective-permute-start(f32[1,128,128]{2,1,0:T(8,128)S(1)} %add.6._.own), channel_id=1, source_target_pairs={{0,2},{1,3},{2,0},{3,1},{4,6},{5,7},{6,4},{7,5},{8,10},{9,11},{10,... | collective-permute-start | bytes 196616 | tf_op jit(solution)/shard_map/ppermute | solution.py:341
  49.1 6.9 %collective-permute-start.16 = (f32[2,128,256]{2,1,0:T(8,128)S(1)}, f32[2,128,256]{2,1,0:T(8,128)S(1)}, u32[]{:S(2)}, u32[]{:S(2)}) collective-permute-start(f32[2,128,256]{2,1,0:T(8,128)S(1)} %get-tuple-element.31), channel_id=1, source_target_pairs={{4,8},{8,4},{12,16},{16,12},{20,24},{24,20},{5,9},{9,5},{13,17},{1... | collective-permute-start | bytes 786440 | tf_op jit(solution)/shard_map/ppermute | solution.py:371
  51.4 4.6 %collective-permute-start.18 = (f32[1,128,128]{2,1,0:T(8,128)S(1)}, f32[1,128,128]{2,1,0:T(8,128)S(1)}, u32[]{:S(2)}, u32[]{:S(2)}) collective-permute-start(f32[1,128,128]{2,1,0:T(8,128)S(1)} %add.7.refs_0_), channel_id=1, source_target_pairs={{0,1},{1,0},{2,3},{3,2},{4,5},{5,4},{6,7},{7,6},{8,9},{9,8},{10,11... | collective-permute-start | bytes 196616 | tf_op jit(solution)/shard_map/ppermute | solution.py:341
  53.0 9.3 %collective-permute-start.15 = (f32[2,128,256]{2,1,0:T(8,128)S(1)}, f32[2,128,256]{2,1,0:T(8,128)S(1)}, u32[]{:S(2)}, u32[]{:S(2)}) collective-permute-start(f32[2,128,256]{2,1,0:T(8,128)S(1)} %get-tuple-element.30), channel_id=1, source_target_pairs={{0,4},{4,0},{8,12},{12,8},{16,20},{20,16},{24,28},{28,24},{1,5},{5... | collective-permute-start | bytes 786440 | tf_op jit(solution)/shard_map/ppermute | solution.py:371
  56.0 8.1 %collective-permute-start.21 = (f32[2,128,128]{2,1,0:T(8,128)S(1)}, f32[2,128,128]{2,1,0:T(8,128)S(1)}, u32[]{:S(2)}, u32[]{:S(2)}) collective-permute-start(f32[2,128,128]{2,1,0:T(8,128)S(1)} %after.2.refs_0_), channel_id=1, source_target_pairs={{0,24},{4,28},{8,16},{12,20},{16,8},{20,12},{24,0},{28,4},{1,25},{... | collective-permute-start | bytes 393224 | tf_op jit(solution)/shard_map/ppermute | solution.py:341
  60.2 6.4 %collective-permute-start.20 = (f32[2,128,128]{2,1,0:T(8,128)S(1)}, f32[2,128,128]{2,1,0:T(8,128)S(1)}, u32[]{:S(2)}, u32[]{:S(2)}) collective-permute-start(f32[2,128,128]{2,1,0:T(8,128)S(1)} %after.2.refs_0_), channel_id=1, source_target_pairs={{0,8},{4,12},{8,0},{12,4},{16,24},{20,28},{24,16},{28,20},{1,9},{5... | collective-permute-start | bytes 393224 | tf_op jit(solution)/shard_map/ppermute | solution.py:341
  62.3 5.1 %collective-permute-start.19 = (f32[2,128,128]{2,1,0:T(8,128)S(1)}, f32[2,128,128]{2,1,0:T(8,128)S(1)}, u32[]{:S(2)}, u32[]{:S(2)}) collective-permute-start(f32[2,128,128]{2,1,0:T(8,128)S(1)} %after.2.refs_0_), channel_id=1, source_target_pairs={{0,16},{4,20},{8,24},{12,28},{16,0},{20,4},{24,8},{28,12},{1,17},{... | collective-permute-start | bytes 393224 | tf_op jit(solution)/shard_map/ppermute | solution.py:341
  67.4 2.0 %collective-permute-start.22 = (f32[8,128,128]{2,1,0:T(8,128)S(1)}, f32[8,128,128]{2,1,0:T(8,128)S(1)}, u32[]{:S(2)}, u32[]{:S(2)}) collective-permute-start(f32[8,128,128]{2,1,0:T(8,128)S(1)} %after.3.refs_0_), channel_id=1, source_target_pairs={{0,4},{4,0},{8,12},{12,8},{16,20},{20,16},{24,28},{28,24},{1,5},{5... | collective-permute-start | bytes 1572872 | tf_op jit(solution)/shard_map/ppermute | solution.py:371

commit v2 on v1

--- a/solution.py
+++ b/solution.py
@@ -12,7 +12,7 @@
 
 FLOOR = 0.5
 LANES = 128
-CHUNK = 32
+CHUNK = 64
 HEAVY = 0
 AHEAD = 4_000_000_000
 AROUND = 2_000_000_000
@@ -129,8 +129,8 @@
 
 def slots_kernel(
     scalars, center, core_tile, far_rows, inner_side, outer_side, inner_near, outer_near, probe, root, tables,
-    probe_sent, probe_keep, inner_side_out, outer_side_out, grad_mid,
-    pad, grid, patch, rows_high, rows_low, freq, sums,
+    sums, inner_side_out, outer_side_out, grad_mid,
+    pad, grid, patch, rows_high, rows_low, freq,
 ):
     half = LANES
     modes = probe.shape[1]
@@ -152,6 +152,8 @@
     pad[:, outer, near, :] = outer_near[...]
     pad[:, :, far, :] = far_rows[...]
     grid[...] = jnp.zeros_like(grid)
+    code = own_code(digit_groups())
+    piece_rows = sums.shape[1]
     sums[...] = jnp.zeros_like(sums)
     lane = lax.broadcasted_iota(jnp.int32, (CHUNK, half), 1)
 
@@ -260,8 +262,8 @@
                         pi = probe[1, m, here, b * half : (b + 1) * half]
                         total[0][b] += pr * br + pi * bi
                         total[1][b] += pr * bi - pi * br
-                        sums[pl.ds(((b * 2 + 0) * modes + m) * length + rows, CHUNK), :] += xr * br + xi * bi
-                        sums[pl.ds(((b * 2 + 1) * modes + m) * length + rows, CHUNK), :] += xr * bi - xi * br
+                        sums[((((b * 2 + 0) * modes + m) * length + rows) // piece_rows) ^ code, pl.ds(rows % piece_rows, CHUNK), :] += xr * br + xi * bi
+                        sums[((((b * 2 + 1) * modes + m) * length + rows) // piece_rows) ^ code, pl.ds(rows % piece_rows, CHUNK), :] += xr * bi - xi * br
                 for c in range(2):
                     ra = pltpu.roll(total[c][0], fore_shift, 1)
                     rb = pltpu.roll(total[c][1], fore_shift, 1)
@@ -274,16 +276,6 @@
 
     lax.fori_loop(0, scalars[0], slot_step, 0)
 
-    kept, rows, _ = probe_keep.shape
-    code = own_code(digit_groups())
-
-    def place_piece(place, carry):
-        for first, target in ((0, probe_keep), (kept, probe_sent)):
-            piece = (place + first) ^ code
-            target[place] = sums[pl.ds(pl.multiple_of(piece * rows, rows), rows), :]
-        return carry
-
-    lax.fori_loop(0, kept, place_piece, 0)
     inner_side_out[...] = grid[:, inner]
     outer_side_out[...] = grid[:, outer]
     for b in range(2):
@@ -461,11 +453,10 @@
     (far_rows,) = call(far_kernel, "far", [shape(2, 4, margin, half)], (chip_rows, inner_corner, outer_corner), weight=AHEAD)
     pieces = 1 << sum(len(bits) for _, bits in groups)
     rows = 2 * 2 * modes * pattern // pieces
-    kept = shape(pieces // 2, rows, half)
-    probe_sent, value, inner_side, outer_side, grad_mid = call(
+    value, inner_side, outer_side, grad_mid = call(
         slots_kernel,
         "slots",
-        [kept, kept, tall_side, tall_side, shape(2, length + 2 * margin, length)],
+        [shape(pieces, rows, half), tall_side, tall_side, shape(2, length + 2 * margin, length)],
         (
             scalars, center, core_tile, far_rows, inner_side, outer_side, inner_near, outer_near,
             probe_modes, root, tables,
@@ -478,12 +469,11 @@
             pltpu.VMEM((modes, 2, pattern, pattern), bf16),
             pltpu.VMEM((modes, 2, pattern, pattern), bf16),
             pltpu.VMEM((modes, 2, pattern, pattern), f32),
-            pltpu.VMEM((2 * 2 * modes * pattern, half), f32),
         ),
         limit=VMEM_LIMIT,
     )
 
-    value = added(value, [paired(probe_sent, "ty", "inner")], weight=HEAVY)
+    value = added(value, [paired(value[pieces // 2 :], "ty", "inner")], weight=HEAVY)
     inner_side = paired(inner_side, "tx", "inner")
     outer_side = paired(outer_side, "tx", "outer")
     for group in groups[1:-1]:

time: 70.3 us -> 72 us (1.024)
    ppermute x9, starting transfers between devices: 18.1 us -> 21.1 us  [exchanged(): lax.ppermute(value, axis, [(i, i ^ mask) for i in range(lax.axis_size(axi...]
    ppermute x14, starting transfers between devices: 21.3 us -> 18.9 us  [paired(): lax.ppermute(value, axis, [(i, j) for i, j in pairs if 0 <= j < count])]
where the time goes in v2:
time: 72 us; the launch traced here: 71.5 us
  starting transfers between devices  40.1 us (56%)
  waiting for transfers between devices  20.1 us (28%)
  Pallas kernels  8.72 us (12%)
  local copies, waits for them, and re-layouts  1.74 us (2%)
  between operations  0.88 us (1%)
    ppermute x9, starting transfers between devices, exchanged(): lax.ppermute(value, axis, [(i, i ^ mask) for i in range(lax.axis_size(axi...  21.1 us
    ppermute x14, starting transfers between devices, paired(): lax.ppermute(value, axis, [(i, j) for i, j in pairs if 0 <= j < count])  18.9 us
    ppermute x9, waiting for transfers between devices, exchanged(): lax.ppermute(value, axis, [(i, i ^ mask) for i in range(lax.axis_size(axi...  18.7 us
    pallas_call x18, Pallas kernels, call(): pl.pallas_call(body, out_shape=tuple(out), in_specs=specs(spaces, len(ope...  8.72 us
    unnamed x12, local copies, waits for them, and re-layouts  1.67 us
  transfers between devices with their start and end apart: 23, of which 12 were waited for; matrix products, arithmetic and copies ran while one was open for 0% of the time, Pallas kernels for 6%

profile of v2, /device:TPU:0, one launch (start us, length us, event | category | flops | bytes accessed | tf_op | source)
XLA Modules:
  0.0 71.5 jit_solution(16949307308665209848)
XLA Ops:
  0.6 0.5 collective-permute-start
  1.1 1.0 %copy-done.2 = f32[2,256,256]{2,1,0:T(8,128)S(1)} copy-done((f32[2,256,256]{2,1,0:T(8,128)S(1)}, f32[2,256,256]{2,1,0:T(8,128)}, u32[]{:S(2)}) %copy-start.2) | copy-done | bytes 524312
  2.2 0.0 copy-start.3
  2.2 0.8 %collective-permute-start.1 = (f32[2,128,256]{2,1,0:T(8,128)S(1)}, f32[2,128,256]{2,1,0:T(8,128)S(1)}, u32[]{:S(2)}, u32[]{:S(2)}) collective-permute-start(f32[2,128,256]{2,1,0:T(8,128)S(1)} %chip_edges.1._), channel_id=1, source_target_pairs={{4,8},{8,4},{12,16},{16,12},{20,24},{24,20},{5,9},{9,5},{13,17},{1... | collective-permute-start | bytes 786440 | tf_op jit(solution)/shard_map/ppermute | solution.py:363
  3.1 0.1 edges.1
  3.2 2.6 %collective-permute-start.4 = (f32[2,256,128]{2,1,0:T(8,128)S(1)}, f32[2,256,128]{2,1,0:T(8,128)S(1)}, u32[]{:S(2)}, u32[]{:S(2)}) collective-permute-start(f32[2,256,128]{2,1,0:T(8,128)S(1)} %get-tuple-element.19), channel_id=1, source_target_pairs={{0,1},{1,0},{2,3},{3,2},{4,5},{5,4},{6,7},{7,6},{8,9},{9,8},{10,11... | collective-permute-start | bytes 786440 | tf_op jit(solution)/shard_map/ppermute | solution.py:363
  5.8 0.7 collective-permute-start.5
  6.5 0.0 copy-done.3
  6.5 0.0 copy-start.4
  6.5 0.0 copy-start.5
  6.5 0.6 root.1._
  7.1 0.1 copy-done.4
  7.2 0.0 copy-done.5
  7.2 1.2 %places.1.__.scalars = s32[7]{0:T(128)S(1)} custom-call(s32[4,8]{1,0:T(4,128)S(1)} %bitcast.6, s32[2,3]{1,0:T(2,128)S(1)} %bitcast.7), custom_call_target="tpu_custom_call" | custom-call | flops 2000000000 | bytes 180 | tf_op jit(solution)/shard_map/places/pallas_call | solution.py:398
  8.4 0.0 collective-permute-done.1.chip_rows
  8.5 4.4 %collective-permute-start.2 = (f32[2,128,128]{2,1,0:T(8,128)S(1)}, f32[2,128,128]{2,1,0:T(8,128)S(1)}, u32[]{:S(2)}, u32[]{:S(2)}) collective-permute-start(f32[2,128,128]{2,1,0:T(8,128)S(1)} %get-tuple-element.17), channel_id=1, source_target_pairs={{0,1},{1,0},{2,3},{3,2},{4,5},{5,4},{6,7},{7,6},{8,9},{9,8},{10,11... | collective-permute-start | bytes 393224 | tf_op jit(solution)/shard_map/ppermute | solution.py:363
  12.9 0.7 collective-permute-start.3
  13.6 0.0 collective-permute-done.4.inner_side
  13.6 0.0 collective-permute-done.5.outer_side
  13.6 2.9 %collective-permute-start.6 = (f32[2,128,128]{2,1,0:T(8,128)S(1)}, f32[2,128,128]{2,1,0:T(8,128)S(1)}, u32[]{:S(2)}, u32[]{:S(2)}) collective-permute-start(f32[2,128,128]{2,1,0:T(8,128)S(1)} %get-tuple-element.21), channel_id=1, source_target_pairs={{0,4},{4,0},{8,12},{12,8},{16,20},{20,16},{24,28},{28,24},{1,5},{5... | collective-permute-start | bytes 393224 | tf_op jit(solution)/shard_map/ppermute | solution.py:363
  16.6 0.1 collective-permute-start.7
  16.7 0.0 collective-permute-done.2.inner_corner
  16.7 0.0 collective-permute-done.3.outer_corner
  16.7 0.8 %collective-permute-done.6.inner_near = f32[2,128,128]{2,1,0:T(8,128)S(1)} collective-permute-done((f32[2,128,128]{2,1,0:T(8,128)S(1)}, f32[2,128,128]{2,1,0:T(8,128)S(1)}, u32[]{:S(2)}, u32[]{:S(2)}) %collective-permute-start.6) | collective-permute-done | bytes 131104 | tf_op jit(solution)/shard_map/ppermute | solution.py:363
  17.5 0.4 collective-permute-done.7.outer_near
  17.9 0.0 collective-permute-done.core_tile
  17.9 0.2 copy-done
  18.2 0.3 copy-done.1
  18.4 3.9 %slots.1 = (f32[16,128,128]{2,1,0:T(8,128)S(1)}, f32[2,512,128]{2,1,0:T(8,128)S(1)}, f32[2,512,128]{2,1,0:T(8,128)S(1)}, f32[2,512,256]{2,1,0:T(8,128)S(1)}) custom-call(s32[7]{0:T(128)S(1)} %places.1.__.scalars, f32[2,256,256]{2,1,0:T(8,128)S(1)} %get-tuple-element.16.center, f32[2,256,256]{2,1,0:T(8,128)S(1)} %collective-permute-done.core_tile, ...), custom_call_target="tpu_custom_call" | custom-call | bytes 9437212 | tf_op jit(solution)/shard_map/slots/pallas_call | solution.py:398
  22.4 0.1 collective-permute-start.10
  22.4 4.6 %collective-permute-start.8 = (f32[2,512,128]{2,1,0:T(8,128)S(1)}, f32[2,512,128]{2,1,0:T(8,128)S(1)}, u32[]{:S(2)}, u32[]{:S(2)}) collective-permute-start(f32[2,512,128]{2,1,0:T(8,128)S(1)} %get-tuple-element.24), channel_id=1, source_target_pairs={{0,1},{1,0},{2,3},{3,2},{4,5},{5,4},{6,7},{7,6},{8,9},{9,8},{10,11... | collective-permute-start | bytes 1572872 | tf_op jit(solution)/shard_map/ppermute | solution.py:363
  27.0 0.7 collective-permute-start.9
  27.7 0.0 collective-permute-done.10.refs_0_
  27.7 0.1 add.4.own
  27.8 8.4 %collective-permute-start.13 = (f32[2,128,128]{2,1,0:T(8,128)S(1)}, f32[2,128,128]{2,1,0:T(8,128)S(1)}, u32[]{:S(2)}, u32[]{:S(2)}) collective-permute-start(f32[2,128,128]{2,1,0:T(8,128)S(1)} %get-tuple-element.30), channel_id=1, source_target_pairs={{0,24},{4,28},{8,16},{12,20},{16,8},{20,12},{24,0},{28,4},{1,25},{... | collective-permute-start | bytes 393224 | tf_op jit(solution)/shard_map/ppermute | solution.py:333
  36.2 0.0 collective-permute-start.12
  36.2 0.6 collective-permute-start.11
  36.9 3.6 %collective-permute-done.13.refs_2_ = f32[2,128,128]{2,1,0:T(8,128)S(1)} collective-permute-done((f32[2,128,128]{2,1,0:T(8,128)S(1)}, f32[2,128,128]{2,1,0:T(8,128)S(1)}, u32[]{:S(2)}, u32[]{:S(2)}) %collective-permute-start.13) | collective-permute-done | bytes 131104 | tf_op jit(solution)/shard_map/ppermute | solution.py:333
  40.5 1.6 %collective-permute-done.12.refs_1_ = f32[2,128,128]{2,1,0:T(8,128)S(1)} collective-permute-done((f32[2,128,128]{2,1,0:T(8,128)S(1)}, f32[2,128,128]{2,1,0:T(8,128)S(1)}, u32[]{:S(2)}, u32[]{:S(2)}) %collective-permute-start.12) | collective-permute-done | bytes 131104 | tf_op jit(solution)/shard_map/ppermute | solution.py:333
  42.2 0.7 collective-permute-done.11.refs_0_
  42.9 1.6 %collective-permute-start.14 = (f32[1,128,128]{2,1,0:T(8,128)S(1)}, f32[1,128,128]{2,1,0:T(8,128)S(1)}, u32[]{:S(2)}, u32[]{:S(2)}) collective-permute-start(f32[1,128,128]{2,1,0:T(8,128)S(1)} %slice.23), channel_id=1, source_target_pairs={{0,1},{1,0},{2,3},{3,2},{4,5},{5,4},{6,7},{7,6},{8,9},{9,8},{10,11... | collective-permute-start | bytes 196616 | tf_op jit(solution)/shard_map/ppermute | solution.py:333
  44.5 2.8 %collective-permute-done.14.refs_0_ = f32[1,128,128]{2,1,0:T(8,128)S(1)} collective-permute-done((f32[1,128,128]{2,1,0:T(8,128)S(1)}, f32[1,128,128]{2,1,0:T(8,128)S(1)}, u32[]{:S(2)}, u32[]{:S(2)}) %collective-permute-start.14) | collective-permute-done | bytes 65568 | tf_op jit(solution)/shard_map/ppermute | solution.py:333
  47.3 2.8 %collective-permute-start.17 = (f32[1,128,128]{2,1,0:T(8,128)S(1)}, f32[1,128,128]{2,1,0:T(8,128)S(1)}, u32[]{:S(2)}, u32[]{:S(2)}) collective-permute-start(f32[1,128,128]{2,1,0:T(8,128)S(1)} %add.6._.own), channel_id=1, source_target_pairs={{0,2},{1,3},{2,0},{3,1},{4,6},{5,7},{6,4},{7,5},{8,10},{9,11},{10,... | collective-permute-start | bytes 196616 | tf_op jit(solution)/shard_map/ppermute | solution.py:333
  50.0 0.0 collective-permute-done.8.inner_side
  50.0 0.0 collective-permute-done.9.outer_side
  50.0 0.1 rows.1
  50.2 0.7 collective-permute-start.16
  50.8 1.7 %collective-permute-done.17.refs_0_ = f32[1,128,128]{2,1,0:T(8,128)S(1)} collective-permute-done((f32[1,128,128]{2,1,0:T(8,128)S(1)}, f32[1,128,128]{2,1,0:T(8,128)S(1)}, u32[]{:S(2)}, u32[]{:S(2)}) %collective-permute-start.17) | collective-permute-done | bytes 65568 | tf_op jit(solution)/shard_map/ppermute | solution.py:333
  52.5 1.6 %collective-permute-start.18 = (f32[1,128,128]{2,1,0:T(8,128)S(1)}, f32[1,128,128]{2,1,0:T(8,128)S(1)}, u32[]{:S(2)}, u32[]{:S(2)}) collective-permute-start(f32[1,128,128]{2,1,0:T(8,128)S(1)} %add.7.refs_0_), channel_id=1, source_target_pairs={{0,1},{1,0},{2,3},{3,2},{4,5},{5,4},{6,7},{7,6},{8,9},{9,8},{10,11... | collective-permute-start | bytes 196616 | tf_op jit(solution)/shard_map/ppermute | solution.py:333
  54.1 0.1 collective-permute-start.15
  54.1 3.0 %collective-permute-done.18.refs_1_ = f32[1,128,128]{2,1,0:T(8,128)S(1)} collective-permute-done((f32[1,128,128]{2,1,0:T(8,128)S(1)}, f32[1,128,128]{2,1,0:T(8,128)S(1)}, u32[]{:S(2)}, u32[]{:S(2)}) %collective-permute-start.18) | collective-permute-done | bytes 65568 | tf_op jit(solution)/shard_map/ppermute | solution.py:333
  57.1 0.0 collective-permute-done.16.chip_in._
  57.1 4.4 %collective-permute-start.21 = (f32[2,128,128]{2,1,0:T(8,128)S(1)}, f32[2,128,128]{2,1,0:T(8,128)S(1)}, u32[]{:S(2)}, u32[]{:S(2)}) collective-permute-start(f32[2,128,128]{2,1,0:T(8,128)S(1)} %after.2.refs_0_), channel_id=1, source_target_pairs={{0,24},{4,28},{8,16},{12,20},{16,8},{20,12},{24,0},{28,4},{1,25},{... | collective-permute-start | bytes 393224 | tf_op jit(solution)/shard_map/ppermute | solution.py:333
  61.5 1.9 %collective-permute-start.20 = (f32[2,128,128]{2,1,0:T(8,128)S(1)}, f32[2,128,128]{2,1,0:T(8,128)S(1)}, u32[]{:S(2)}, u32[]{:S(2)}) collective-permute-start(f32[2,128,128]{2,1,0:T(8,128)S(1)} %after.2.refs_0_), channel_id=1, source_target_pairs={{0,8},{4,12},{8,0},{12,4},{16,24},{20,28},{24,16},{28,20},{1,9},{5... | collective-permute-start | bytes 393224 | tf_op jit(solution)/shard_map/ppermute | solution.py:333
  63.3 0.0 collective-permute-start.19
  63.3 0.0 collective-permute-done.15.core_in._
  63.3 1.8 %collective-permute-done.21.refs_3_ = f32[2,128,128]{2,1,0:T(8,128)S(1)} collective-permute-done((f32[2,128,128]{2,1,0:T(8,128)S(1)}, f32[2,128,128]{2,1,0:T(8,128)S(1)}, u32[]{:S(2)}, u32[]{:S(2)}) %collective-permute-start.21) | collective-permute-done | bytes 131104 | tf_op jit(solution)/shard_map/ppermute | solution.py:333
  65.2 2.6 %collective-permute-done.20.refs_2_ = f32[2,128,128]{2,1,0:T(8,128)S(1)} collective-permute-done((f32[2,128,128]{2,1,0:T(8,128)S(1)}, f32[2,128,128]{2,1,0:T(8,128)S(1)}, u32[]{:S(2)}, u32[]{:S(2)}) %collective-permute-start.20) | collective-permute-done | bytes 131104 | tf_op jit(solution)/shard_map/ppermute | solution.py:333
  67.7 0.9 %collective-permute-done.19.refs_1_ = f32[2,128,128]{2,1,0:T(8,128)S(1)} collective-permute-done((f32[2,128,128]{2,1,0:T(8,128)S(1)}, f32[2,128,128]{2,1,0:T(8,128)S(1)}, u32[]{:S(2)}, u32[]{:S(2)}) %collective-permute-start.19) | collective-permute-done | bytes 131104 | tf_op jit(solution)/shard_map/ppermute | solution.py:333
  68.7 0.1 collective-permute-start.22
  68.8 0.9 %columns.1 = f32[2,256,256]{2,1,0:T(8,128)} custom-call(f32[2,256,256]{2,1,0:T(8,128)S(1)} %get-tuple-element.27.inner_grad, f32[2,128,256]{2,1,0:T(8,128)S(1)} %collective-permute-done.15.core_in._, f32[2,128,256]{2,1,0:T(8,128)S(1)} %collective-permute-done.16.chip_in._), custom_call_target="tpu_custom_call" | custom-call | bytes 1572864 | tf_op jit(solution)/shard_map/columns/pallas_call | solution.py:398
  69.6 0.8 %join.1.refs_1_ = f32[2,2,256,256]{3,2,1,0:T(8,128)} custom-call(f32[8,128,128]{2,1,0:T(8,128)S(1)} %after.3.refs_0_), custom_call_target="tpu_custom_call" | custom-call | flops 2000000000 | bytes 1572864 | tf_op jit(solution)/shard_map/join/pallas_call | solution.py:398
  70.5 0.2 collective-permute-done.22.refs_0_
  70.7 0.8 %join_rest.1 = f32[2,2,256,256]{3,2,1,0:T(8,128)} custom-call(f32[8,128,128]{2,1,0:T(8,128)S(1)} %collective-permute-done.22.refs_0_, f32[2,2,256,256]{3,2,1,0:T(8,128)} %join.1.refs_1_), custom_call_target="tpu_custom_call", output_to_operand_aliasing={{}: (1, {})} | custom-call | bytes 2621440 | tf_op jit(solution)/shard_map/join_rest/pallas_call | solution.py:398
  (15 shorter events, 0.3 us)
Async XLA Ops:
  0.6 17.3 %collective-permute-start = (f32[2,256,256]{2,1,0:T(8,128)}, f32[2,256,256]{2,1,0:T(8,128)S(1)}, u32[]{:S(2)}, u32[]{:S(2)}) collective-permute-start(f32[2,256,256]{2,1,0:T(8,128)} %field.3), channel_id=1, source_target_pairs={{0,4},{4,0},{8,12},{12,8},{16,20},{20,16},{24,28},{28,24},{1,5},{5... | collective-permute-start | bytes 1572872 | tf_op jit(solution)/shard_map/ppermute | solution.py:363
  1.1 1.0 %copy-start.2 = (f32[2,256,256]{2,1,0:T(8,128)S(1)}, f32[2,256,256]{2,1,0:T(8,128)}, u32[]{:S(2)}) copy-start(f32[2,256,256]{2,1,0:T(8,128)} %field.3) | copy-start | bytes 1572868
  2.2 4.3 %copy-start.3 = (f32[1,1,3,256,256]{4,3,2,1,0:T(8,128)S(1)}, f32[1,1,3,256,256]{4,3,2,1,0:T(8,128)}, u32[]{:S(2)}) copy-start(f32[1,1,3,256,256]{4,3,2,1,0:T(8,128)} %param.8) | copy-start | bytes 2359300
  2.2 6.2 %collective-permute-start.1 = (f32[2,128,256]{2,1,0:T(8,128)S(1)}, f32[2,128,256]{2,1,0:T(8,128)S(1)}, u32[]{:S(2)}, u32[]{:S(2)}) collective-permute-start(f32[2,128,256]{2,1,0:T(8,128)S(1)} %chip_edges.1._), channel_id=1, source_target_pairs={{4,8},{8,4},{12,16},{16,12},{20,24},{24,20},{5,9},{9,5},{13,17},{1... | collective-permute-start | bytes 786440 | tf_op jit(solution)/shard_map/ppermute | solution.py:363
  3.2 10.4 %collective-permute-start.4 = (f32[2,256,128]{2,1,0:T(8,128)S(1)}, f32[2,256,128]{2,1,0:T(8,128)S(1)}, u32[]{:S(2)}, u32[]{:S(2)}) collective-permute-start(f32[2,256,128]{2,1,0:T(8,128)S(1)} %get-tuple-element.19), channel_id=1, source_target_pairs={{0,1},{1,0},{2,3},{3,2},{4,5},{5,4},{6,7},{7,6},{8,9},{9,8},{10,11... | collective-permute-start | bytes 786440 | tf_op jit(solution)/shard_map/ppermute | solution.py:363
  5.8 7.8 %collective-permute-start.5 = (f32[2,256,128]{2,1,0:T(8,128)S(1)}, f32[2,256,128]{2,1,0:T(8,128)S(1)}, u32[]{:S(2)}, u32[]{:S(2)}) collective-permute-start(f32[2,256,128]{2,1,0:T(8,128)S(1)} %get-tuple-element.20), channel_id=1, source_target_pairs={{1,2},{2,1},{5,6},{6,5},{9,10},{10,9},{13,14},{14,13},{17,18},{18,... | collective-permute-start | bytes 786440 | tf_op jit(solution)/shard_map/ppermute | solution.py:363
  6.5 0.7 copy-start.4
  6.5 0.7 copy-start.5
  8.5 8.2 %collective-permute-start.2 = (f32[2,128,128]{2,1,0:T(8,128)S(1)}, f32[2,128,128]{2,1,0:T(8,128)S(1)}, u32[]{:S(2)}, u32[]{:S(2)}) collective-permute-start(f32[2,128,128]{2,1,0:T(8,128)S(1)} %get-tuple-element.17), channel_id=1, source_target_pairs={{0,1},{1,0},{2,3},{3,2},{4,5},{5,4},{6,7},{7,6},{8,9},{9,8},{10,11... | collective-permute-start | bytes 393224 | tf_op jit(solution)/shard_map/ppermute | solution.py:363
  12.9 3.8 %collective-permute-start.3 = (f32[2,128,128]{2,1,0:T(8,128)S(1)}, f32[2,128,128]{2,1,0:T(8,128)S(1)}, u32[]{:S(2)}, u32[]{:S(2)}) collective-permute-start(f32[2,128,128]{2,1,0:T(8,128)S(1)} %get-tuple-element.18), channel_id=1, source_target_pairs={{1,2},{2,1},{5,6},{6,5},{9,10},{10,9},{13,14},{14,13},{17,18},{18,... | collective-permute-start | bytes 393224 | tf_op jit(solution)/shard_map/ppermute | solution.py:363
  13.6 3.9 %collective-permute-start.6 = (f32[2,128,128]{2,1,0:T(8,128)S(1)}, f32[2,128,128]{2,1,0:T(8,128)S(1)}, u32[]{:S(2)}, u32[]{:S(2)}) collective-permute-start(f32[2,128,128]{2,1,0:T(8,128)S(1)} %get-tuple-element.21), channel_id=1, source_target_pairs={{0,4},{4,0},{8,12},{12,8},{16,20},{20,16},{24,28},{28,24},{1,5},{5... | collective-permute-start | bytes 393224 | tf_op jit(solution)/shard_map/ppermute | solution.py:363
  16.6 1.6 %copy-start = (bf16[8,2,256,256]{3,2,1,0:T(8,128)(2,1)S(1)}, bf16[8,2,256,256]{3,2,1,0:T(8,128)(2,1)}, u32[]{:S(2)}) copy-start(bf16[8,2,256,256]{3,2,1,0:T(8,128)(2,1)} %constant.2.clone.tables) | copy-start | bytes 6291460
  16.6 1.9 %copy-start.1 = (f32[2,2,256,256]{3,2,1,0:T(8,128)S(1)}, f32[2,2,256,256]{3,2,1,0:T(8,128)}, u32[]{:S(2)}) copy-start(f32[2,2,256,256]{3,2,1,0:T(8,128)} %probe.1) | copy-start | bytes 3145732
  16.6 1.3 %collective-permute-start.7 = (f32[2,128,128]{2,1,0:T(8,128)S(1)}, f32[2,128,128]{2,1,0:T(8,128)S(1)}, u32[]{:S(2)}, u32[]{:S(2)}) collective-permute-start(f32[2,128,128]{2,1,0:T(8,128)S(1)} %get-tuple-element.22), channel_id=1, source_target_pairs={{0,4},{4,0},{8,12},{12,8},{16,20},{20,16},{24,28},{28,24},{1,5},{5... | collective-permute-start | bytes 393224 | tf_op jit(solution)/shard_map/ppermute | solution.py:363
  22.4 5.4 %collective-permute-start.10 = (f32[8,128,128]{2,1,0:T(8,128)S(1)}, f32[8,128,128]{2,1,0:T(8,128)S(1)}, u32[]{:S(2)}, u32[]{:S(2)}) collective-permute-start(f32[8,128,128]{2,1,0:T(8,128)S(1)} %slice.15), channel_id=1, source_target_pairs={{0,4},{4,0},{8,12},{12,8},{16,20},{20,16},{24,28},{28,24},{1,5},{5... | collective-permute-start | bytes 1572872 | tf_op jit(solution)/shard_map/ppermute | solution.py:363
  22.4 27.6 %collective-permute-start.8 = (f32[2,512,128]{2,1,0:T(8,128)S(1)}, f32[2,512,128]{2,1,0:T(8,128)S(1)}, u32[]{:S(2)}, u32[]{:S(2)}) collective-permute-start(f32[2,512,128]{2,1,0:T(8,128)S(1)} %get-tuple-element.24), channel_id=1, source_target_pairs={{0,1},{1,0},{2,3},{3,2},{4,5},{5,4},{6,7},{7,6},{8,9},{9,8},{10,11... | collective-permute-start | bytes 1572872 | tf_op jit(solution)/shard_map/ppermute | solution.py:363
  27.0 23.0 %collective-permute-start.9 = (f32[2,512,128]{2,1,0:T(8,128)S(1)}, f32[2,512,128]{2,1,0:T(8,128)S(1)}, u32[]{:S(2)}, u32[]{:S(2)}) collective-permute-start(f32[2,512,128]{2,1,0:T(8,128)S(1)} %get-tuple-element.25), channel_id=1, source_target_pairs={{1,2},{2,1},{5,6},{6,5},{9,10},{10,9},{13,14},{14,13},{17,18},{18,... | collective-permute-start | bytes 1572872 | tf_op jit(solution)/shard_map/ppermute | solution.py:363
  27.8 12.7 %collective-permute-start.13 = (f32[2,128,128]{2,1,0:T(8,128)S(1)}, f32[2,128,128]{2,1,0:T(8,128)S(1)}, u32[]{:S(2)}, u32[]{:S(2)}) collective-permute-start(f32[2,128,128]{2,1,0:T(8,128)S(1)} %get-tuple-element.30), channel_id=1, source_target_pairs={{0,24},{4,28},{8,16},{12,20},{16,8},{20,12},{24,0},{28,4},{1,25},{... | collective-permute-start | bytes 393224 | tf_op jit(solution)/shard_map/ppermute | solution.py:333
  36.2 5.9 %collective-permute-start.12 = (f32[2,128,128]{2,1,0:T(8,128)S(1)}, f32[2,128,128]{2,1,0:T(8,128)S(1)}, u32[]{:S(2)}, u32[]{:S(2)}) collective-permute-start(f32[2,128,128]{2,1,0:T(8,128)S(1)} %get-tuple-element.31), channel_id=1, source_target_pairs={{0,8},{4,12},{8,0},{12,4},{16,24},{20,28},{24,16},{28,20},{1,9},{5... | collective-permute-start | bytes 393224 | tf_op jit(solution)/shard_map/ppermute | solution.py:333
  36.2 6.6 %collective-permute-start.11 = (f32[2,128,128]{2,1,0:T(8,128)S(1)}, f32[2,128,128]{2,1,0:T(8,128)S(1)}, u32[]{:S(2)}, u32[]{:S(2)}) collective-permute-start(f32[2,128,128]{2,1,0:T(8,128)S(1)} %get-tuple-element.32), channel_id=1, source_target_pairs={{0,16},{4,20},{8,24},{12,28},{16,0},{20,4},{24,8},{28,12},{1,17},{... | collective-permute-start | bytes 393224 | tf_op jit(solution)/shard_map/ppermute | solution.py:333
  42.9 4.3 %collective-permute-start.14 = (f32[1,128,128]{2,1,0:T(8,128)S(1)}, f32[1,128,128]{2,1,0:T(8,128)S(1)}, u32[]{:S(2)}, u32[]{:S(2)}) collective-permute-start(f32[1,128,128]{2,1,0:T(8,128)S(1)} %slice.23), channel_id=1, source_target_pairs={{0,1},{1,0},{2,3},{3,2},{4,5},{5,4},{6,7},{7,6},{8,9},{9,8},{10,11... | collective-permute-start | bytes 196616 | tf_op jit(solution)/shard_map/ppermute | solution.py:333
  47.3 5.2 %collective-permute-start.17 = (f32[1,128,128]{2,1,0:T(8,128)S(1)}, f32[1,128,128]{2,1,0:T(8,128)S(1)}, u32[]{:S(2)}, u32[]{:S(2)}) collective-permute-start(f32[1,128,128]{2,1,0:T(8,128)S(1)} %add.6._.own), channel_id=1, source_target_pairs={{0,2},{1,3},{2,0},{3,1},{4,6},{5,7},{6,4},{7,5},{8,10},{9,11},{10,... | collective-permute-start | bytes 196616 | tf_op jit(solution)/shard_map/ppermute | solution.py:333
  50.2 6.9 %collective-permute-start.16 = (f32[2,128,256]{2,1,0:T(8,128)S(1)}, f32[2,128,256]{2,1,0:T(8,128)S(1)}, u32[]{:S(2)}, u32[]{:S(2)}) collective-permute-start(f32[2,128,256]{2,1,0:T(8,128)S(1)} %get-tuple-element.29), channel_id=1, source_target_pairs={{4,8},{8,4},{12,16},{16,12},{20,24},{24,20},{5,9},{9,5},{13,17},{1... | collective-permute-start | bytes 786440 | tf_op jit(solution)/shard_map/ppermute | solution.py:363
  52.5 4.6 %collective-permute-start.18 = (f32[1,128,128]{2,1,0:T(8,128)S(1)}, f32[1,128,128]{2,1,0:T(8,128)S(1)}, u32[]{:S(2)}, u32[]{:S(2)}) collective-permute-start(f32[1,128,128]{2,1,0:T(8,128)S(1)} %add.7.refs_0_), channel_id=1, source_target_pairs={{0,1},{1,0},{2,3},{3,2},{4,5},{5,4},{6,7},{7,6},{8,9},{9,8},{10,11... | collective-permute-start | bytes 196616 | tf_op jit(solution)/shard_map/ppermute | solution.py:333
  54.1 9.3 %collective-permute-start.15 = (f32[2,128,256]{2,1,0:T(8,128)S(1)}, f32[2,128,256]{2,1,0:T(8,128)S(1)}, u32[]{:S(2)}, u32[]{:S(2)}) collective-permute-start(f32[2,128,256]{2,1,0:T(8,128)S(1)} %get-tuple-element.28), channel_id=1, source_target_pairs={{0,4},{4,0},{8,12},{12,8},{16,20},{20,16},{24,28},{28,24},{1,5},{5... | collective-permute-start | bytes 786440 | tf_op jit(solution)/shard_map/ppermute | solution.py:363
  57.1 8.1 %collective-permute-start.21 = (f32[2,128,128]{2,1,0:T(8,128)S(1)}, f32[2,128,128]{2,1,0:T(8,128)S(1)}, u32[]{:S(2)}, u32[]{:S(2)}) collective-permute-start(f32[2,128,128]{2,1,0:T(8,128)S(1)} %after.2.refs_0_), channel_id=1, source_target_pairs={{0,24},{4,28},{8,16},{12,20},{16,8},{20,12},{24,0},{28,4},{1,25},{... | collective-permute-start | bytes 393224 | tf_op jit(solution)/shard_map/ppermute | solution.py:333
  61.5 6.3 %collective-permute-start.20 = (f32[2,128,128]{2,1,0:T(8,128)S(1)}, f32[2,128,128]{2,1,0:T(8,128)S(1)}, u32[]{:S(2)}, u32[]{:S(2)}) collective-permute-start(f32[2,128,128]{2,1,0:T(8,128)S(1)} %after.2.refs_0_), channel_id=1, source_target_pairs={{0,8},{4,12},{8,0},{12,4},{16,24},{20,28},{24,16},{28,20},{1,9},{5... | collective-permute-start | bytes 393224 | tf_op jit(solution)/shard_map/ppermute | solution.py:333
  63.3 5.3 %collective-permute-start.19 = (f32[2,128,128]{2,1,0:T(8,128)S(1)}, f32[2,128,128]{2,1,0:T(8,128)S(1)}, u32[]{:S(2)}, u32[]{:S(2)}) collective-permute-start(f32[2,128,128]{2,1,0:T(8,128)S(1)} %after.2.refs_0_), channel_id=1, source_target_pairs={{0,16},{4,20},{8,24},{12,28},{16,0},{20,4},{24,8},{28,12},{1,17},{... | collective-permute-start | bytes 393224 | tf_op jit(solution)/shard_map/ppermute | solution.py:333
  68.7 2.0 %collective-permute-start.22 = (f32[8,128,128]{2,1,0:T(8,128)S(1)}, f32[8,128,128]{2,1,0:T(8,128)S(1)}, u32[]{:S(2)}, u32[]{:S(2)}) collective-permute-start(f32[8,128,128]{2,1,0:T(8,128)S(1)} %after.3.refs_0_), channel_id=1, source_target_pairs={{0,4},{4,0},{8,12},{12,8},{16,20},{20,16},{24,28},{28,24},{1,5},{5... | collective-permute-start | bytes 1572872 | tf_op jit(solution)/shard_map/ppermute | solution.py:363

commit v3 on v2

--- a/solution.py
+++ b/solution.py
@@ -85,10 +85,10 @@
         copy.wait()
 
 
-def near_kernel(inner_side, outer_side, inner_near, outer_near):
+def near_kernel(inner_side, outer_side, corners):
     near, _ = near_and_far(LANES)
-    inner_near[...] = inner_side[:, pl.ds(near, LANES), :]
-    outer_near[...] = outer_side[:, pl.ds(near, LANES), :]
+    corners[0] = inner_side[:, pl.ds(near, LANES), :]
+    corners[1] = outer_side[:, pl.ds(near, LANES), :]
 
 
 def far_kernel(chip_rows, inner_corner, outer_corner, far_rows):
@@ -128,7 +128,7 @@
 
 
 def slots_kernel(
-    scalars, center, core_tile, far_rows, inner_side, outer_side, inner_near, outer_near, probe, root, tables,
+    scalars, center, core_tile, far_rows, inner_side, outer_side, near_corners, probe, root, tables,
     sums, inner_side_out, outer_side_out, grad_mid,
     pad, grid, patch, rows_high, rows_low, freq,
 ):
@@ -148,8 +148,8 @@
         pad[:, 1 + b, near, :] = core_tile[:, core_half, cols]
     pad[:, inner, own, :] = inner_side[...]
     pad[:, outer, own, :] = outer_side[...]
-    pad[:, inner, near, :] = inner_near[...]
-    pad[:, outer, near, :] = outer_near[...]
+    pad[:, inner, near, :] = near_corners[0]
+    pad[:, outer, near, :] = near_corners[1]
     pad[:, :, far, :] = far_rows[...]
     grid[...] = jnp.zeros_like(grid)
     code = own_code(digit_groups())
@@ -447,9 +447,8 @@
     inner_corner, outer_corner = call(corners_kernel, "corners", [corner, corner], (chip_rows, root, scalars), "vhh")
     inner_corner = paired(inner_corner, "tx", "inner")
     outer_corner = paired(outer_corner, "tx", "outer")
-    inner_near, outer_near = call(near_kernel, "near", [corner, corner], (inner_side, outer_side))
-    inner_near = paired(inner_near, "ty", "inner")
-    outer_near = paired(outer_near, "ty", "inner")
+    (near_corners,) = call(near_kernel, "near", [shape(2, 2, margin, margin)], (inner_side, outer_side))
+    near_corners = paired(near_corners, "ty", "inner")
     (far_rows,) = call(far_kernel, "far", [shape(2, 4, margin, half)], (chip_rows, inner_corner, outer_corner), weight=AHEAD)
     pieces = 1 << sum(len(bits) for _, bits in groups)
     rows = 2 * 2 * modes * pattern // pieces
@@ -458,7 +457,7 @@
         "slots",
         [shape(pieces, rows, half), tall_side, tall_side, shape(2, length + 2 * margin, length)],
         (
-            scalars, center, core_tile, far_rows, inner_side, outer_side, inner_near, outer_near,
+            scalars, center, core_tile, far_rows, inner_side, outer_side, near_corners,
             probe_modes, root, tables,
         ),
         "s",

time: 72 us -> 69.6 us (0.967)
  starting transfers between devices: 40.1 us -> 38 us
    ppermute x9, starting transfers between devices: 21.1 us -> 18.6 us  [exchanged(): lax.ppermute(value, axis, [(i, i ^ mask) for i in range(lax.axis_size(axi...]
    ppermute x14 -> x13, starting transfers between devices: 18.9 us -> 19.4 us  [paired(): lax.ppermute(value, axis, [(i, j) for i, j in pairs if 0 <= j < count])]
  transfers between devices with their start and end apart: 23 -> 22, of which waited for: 12 -> 11; matrix products, arithmetic and copies ran while one was open for 0% -> 0% of each run, Pallas kernels for 6% -> 6%
where the time goes in v3:
time: 69.6 us; the launch traced here: 69.3 us
  starting transfers between devices  38 us (55%)
  waiting for transfers between devices  20.4 us (29%)
  Pallas kernels  8.74 us (13%)
  local copies, waits for them, and re-layouts  1.25 us (2%)
  between operations  0.9 us (1%)
    ppermute x13, starting transfers between devices, paired(): lax.ppermute(value, axis, [(i, j) for i, j in pairs if 0 <= j < count])  19.4 us
    ppermute x9, waiting for transfers between devices, exchanged(): lax.ppermute(value, axis, [(i, i ^ mask) for i in range(lax.axis_size(axi...  19.1 us
    ppermute x9, starting transfers between devices, exchanged(): lax.ppermute(value, axis, [(i, i ^ mask) for i in range(lax.axis_size(axi...  18.6 us
    pallas_call x18, Pallas kernels, call(): pl.pallas_call(body, out_shape=tuple(out), in_specs=specs(spaces, len(ope...  8.74 us
  transfers between devices with their start and end apart: 22, of which 11 were waited for; matrix products, arithmetic and copies ran while one was open for 0% of the time, Pallas kernels for 6%

profile of v3, /device:TPU:0, one launch (start us, length us, event | category | flops | bytes accessed | tf_op | source)
XLA Modules:
  0.0 69.3 jit_solution(10185231331371974968)
XLA Ops:
  0.6 0.5 collective-permute-start
  1.1 1.0 %copy-done.2 = f32[2,256,256]{2,1,0:T(8,128)S(1)} copy-done((f32[2,256,256]{2,1,0:T(8,128)S(1)}, f32[2,256,256]{2,1,0:T(8,128)}, u32[]{:S(2)}) %copy-start.2) | copy-done | bytes 524312
  2.2 0.0 copy-start.3
  2.2 0.8 %collective-permute-start.1 = (f32[2,128,256]{2,1,0:T(8,128)S(1)}, f32[2,128,256]{2,1,0:T(8,128)S(1)}, u32[]{:S(2)}, u32[]{:S(2)}) collective-permute-start(f32[2,128,256]{2,1,0:T(8,128)S(1)} %chip_edges.1._), channel_id=1, source_target_pairs={{4,8},{8,4},{12,16},{16,12},{20,24},{24,20},{5,9},{9,5},{13,17},{1... | collective-permute-start | bytes 786440 | tf_op jit(solution)/shard_map/ppermute | solution.py:363
  3.1 0.1 edges.1
  3.2 2.6 %collective-permute-start.4 = (f32[2,256,128]{2,1,0:T(8,128)S(1)}, f32[2,256,128]{2,1,0:T(8,128)S(1)}, u32[]{:S(2)}, u32[]{:S(2)}) collective-permute-start(f32[2,256,128]{2,1,0:T(8,128)S(1)} %get-tuple-element.17), channel_id=1, source_target_pairs={{0,1},{1,0},{2,3},{3,2},{4,5},{5,4},{6,7},{7,6},{8,9},{9,8},{10,11... | collective-permute-start | bytes 786440 | tf_op jit(solution)/shard_map/ppermute | solution.py:363
  5.8 0.7 collective-permute-start.5
  6.5 0.0 copy-done.3
  6.5 0.0 copy-start.4
  6.5 0.0 copy-start.5
  6.5 0.6 root.1._
  7.1 0.1 copy-done.4
  7.2 0.0 copy-done.5
  7.2 1.2 %places.1.__.scalars = s32[7]{0:T(128)S(1)} custom-call(s32[4,8]{1,0:T(4,128)S(1)} %bitcast.6, s32[2,3]{1,0:T(2,128)S(1)} %bitcast.7), custom_call_target="tpu_custom_call" | custom-call | flops 2000000000 | bytes 180 | tf_op jit(solution)/shard_map/places/pallas_call | solution.py:398
  8.4 0.0 collective-permute-done.1.chip_rows
  8.5 4.4 %collective-permute-start.2 = (f32[2,128,128]{2,1,0:T(8,128)S(1)}, f32[2,128,128]{2,1,0:T(8,128)S(1)}, u32[]{:S(2)}, u32[]{:S(2)}) collective-permute-start(f32[2,128,128]{2,1,0:T(8,128)S(1)} %get-tuple-element.15), channel_id=1, source_target_pairs={{0,1},{1,0},{2,3},{3,2},{4,5},{5,4},{6,7},{7,6},{8,9},{9,8},{10,11... | collective-permute-start | bytes 393224 | tf_op jit(solution)/shard_map/ppermute | solution.py:363
  12.9 0.7 collective-permute-start.3
  13.6 0.0 collective-permute-done.4.inner_side
  13.6 0.0 collective-permute-done.5.outer_side
  13.6 0.0 copy-start
  13.6 0.0 copy-start.1
  13.7 2.9 %collective-permute-start.6 = (f32[2,2,128,128]{3,2,1,0:T(8,128)S(1)}, f32[2,2,128,128]{3,2,1,0:T(8,128)S(1)}, u32[]{:S(2)}, u32[]{:S(2)}) collective-permute-start(f32[2,2,128,128]{3,2,1,0:T(8,128)S(1)} %near.1), channel_id=1, source_target_pairs={{0,4},{4,0},{8,12},{12,8},{16,20},{20,16},{24,28},{28,24},{1,5},{5... | collective-permute-start | bytes 786440 | tf_op jit(solution)/shard_map/ppermute | solution.py:363
  16.6 0.0 collective-permute-done.2.inner_corner
  16.6 0.0 collective-permute-done.3.outer_corner
  16.6 0.0 collective-permute-done.core_tile
  16.6 1.1 %collective-permute-done.6.near_corners = f32[2,2,128,128]{3,2,1,0:T(8,128)S(1)} collective-permute-done((f32[2,2,128,128]{3,2,1,0:T(8,128)S(1)}, f32[2,2,128,128]{3,2,1,0:T(8,128)S(1)}, u32[]{:S(2)}, u32[]{:S(2)}) %collective-permute-start.6) | collective-permute-done | bytes 262176 | tf_op jit(solution)/shard_map/ppermute | solution.py:363
  17.7 0.0 copy-done
  17.8 0.0 copy-done.1
  17.8 3.9 %slots.1 = (f32[16,128,128]{2,1,0:T(8,128)S(1)}, f32[2,512,128]{2,1,0:T(8,128)S(1)}, f32[2,512,128]{2,1,0:T(8,128)S(1)}, f32[2,512,256]{2,1,0:T(8,128)S(1)}) custom-call(s32[7]{0:T(128)S(1)} %places.1.__.scalars, f32[2,256,256]{2,1,0:T(8,128)S(1)} %get-tuple-element.14.center, f32[2,256,256]{2,1,0:T(8,128)S(1)} %collective-permute-done.core_tile, ...), custom_call_target="tpu_custom_call" | custom-call | bytes 9437212 | tf_op jit(solution)/shard_map/slots/pallas_call | solution.py:398
  21.7 0.6 collective-permute-start.9
  22.4 4.6 %collective-permute-start.7 = (f32[2,512,128]{2,1,0:T(8,128)S(1)}, f32[2,512,128]{2,1,0:T(8,128)S(1)}, u32[]{:S(2)}, u32[]{:S(2)}) collective-permute-start(f32[2,512,128]{2,1,0:T(8,128)S(1)} %get-tuple-element.20), channel_id=1, source_target_pairs={{0,1},{1,0},{2,3},{3,2},{4,5},{5,4},{6,7},{7,6},{8,9},{9,8},{10,11... | collective-permute-start | bytes 1572872 | tf_op jit(solution)/shard_map/ppermute | solution.py:363
  27.0 0.7 collective-permute-start.8
  27.7 0.0 collective-permute-done.9.refs_0_
  27.7 0.1 add.4.own
  27.8 5.5 %collective-permute-start.12 = (f32[2,128,128]{2,1,0:T(8,128)S(1)}, f32[2,128,128]{2,1,0:T(8,128)S(1)}, u32[]{:S(2)}, u32[]{:S(2)}) collective-permute-start(f32[2,128,128]{2,1,0:T(8,128)S(1)} %get-tuple-element.26), channel_id=1, source_target_pairs={{0,24},{4,28},{8,16},{12,20},{16,8},{20,12},{24,0},{28,4},{1,25},{... | collective-permute-start | bytes 393224 | tf_op jit(solution)/shard_map/ppermute | solution.py:333
  33.3 0.0 collective-permute-start.11
  33.3 0.6 collective-permute-start.10
  34.0 3.6 %collective-permute-done.12.refs_2_ = f32[2,128,128]{2,1,0:T(8,128)S(1)} collective-permute-done((f32[2,128,128]{2,1,0:T(8,128)S(1)}, f32[2,128,128]{2,1,0:T(8,128)S(1)}, u32[]{:S(2)}, u32[]{:S(2)}) %collective-permute-start.12) | collective-permute-done | bytes 131104 | tf_op jit(solution)/shard_map/ppermute | solution.py:333
  37.6 1.6 %collective-permute-done.11.refs_1_ = f32[2,128,128]{2,1,0:T(8,128)S(1)} collective-permute-done((f32[2,128,128]{2,1,0:T(8,128)S(1)}, f32[2,128,128]{2,1,0:T(8,128)S(1)}, u32[]{:S(2)}, u32[]{:S(2)}) %collective-permute-start.11) | collective-permute-done | bytes 131104 | tf_op jit(solution)/shard_map/ppermute | solution.py:333
  39.2 0.7 %collective-permute-done.10.refs_0_ = f32[2,128,128]{2,1,0:T(8,128)S(1)} collective-permute-done((f32[2,128,128]{2,1,0:T(8,128)S(1)}, f32[2,128,128]{2,1,0:T(8,128)S(1)}, u32[]{:S(2)}, u32[]{:S(2)}) %collective-permute-start.10) | collective-permute-done | bytes 131104 | tf_op jit(solution)/shard_map/ppermute | solution.py:333
  40.0 3.3 %collective-permute-start.13 = (f32[1,128,128]{2,1,0:T(8,128)S(1)}, f32[1,128,128]{2,1,0:T(8,128)S(1)}, u32[]{:S(2)}, u32[]{:S(2)}) collective-permute-start(f32[1,128,128]{2,1,0:T(8,128)S(1)} %slice.23), channel_id=1, source_target_pairs={{0,1},{1,0},{2,3},{3,2},{4,5},{5,4},{6,7},{7,6},{8,9},{9,8},{10,11... | collective-permute-start | bytes 196616 | tf_op jit(solution)/shard_map/ppermute | solution.py:333
  43.3 2.3 %collective-permute-done.13.refs_0_ = f32[1,128,128]{2,1,0:T(8,128)S(1)} collective-permute-done((f32[1,128,128]{2,1,0:T(8,128)S(1)}, f32[1,128,128]{2,1,0:T(8,128)S(1)}, u32[]{:S(2)}, u32[]{:S(2)}) %collective-permute-start.13) | collective-permute-done | bytes 65568 | tf_op jit(solution)/shard_map/ppermute | solution.py:333
  45.6 1.8 %collective-permute-start.16 = (f32[1,128,128]{2,1,0:T(8,128)S(1)}, f32[1,128,128]{2,1,0:T(8,128)S(1)}, u32[]{:S(2)}, u32[]{:S(2)}) collective-permute-start(f32[1,128,128]{2,1,0:T(8,128)S(1)} %add.6._.own), channel_id=1, source_target_pairs={{0,2},{1,3},{2,0},{3,1},{4,6},{5,7},{6,4},{7,5},{8,10},{9,11},{10,... | collective-permute-start | bytes 196616 | tf_op jit(solution)/shard_map/ppermute | solution.py:333
  47.4 0.0 collective-permute-done.7.inner_side
  47.4 0.0 collective-permute-done.8.outer_side
  47.4 0.1 rows.1
  47.5 0.7 collective-permute-start.15
  48.2 2.6 %collective-permute-done.16.refs_0_ = f32[1,128,128]{2,1,0:T(8,128)S(1)} collective-permute-done((f32[1,128,128]{2,1,0:T(8,128)S(1)}, f32[1,128,128]{2,1,0:T(8,128)S(1)}, u32[]{:S(2)}, u32[]{:S(2)}) %collective-permute-start.16) | collective-permute-done | bytes 65568 | tf_op jit(solution)/shard_map/ppermute | solution.py:333
  50.9 2.0 %collective-permute-start.17 = (f32[1,128,128]{2,1,0:T(8,128)S(1)}, f32[1,128,128]{2,1,0:T(8,128)S(1)}, u32[]{:S(2)}, u32[]{:S(2)}) collective-permute-start(f32[1,128,128]{2,1,0:T(8,128)S(1)} %add.7.refs_0_), channel_id=1, source_target_pairs={{0,1},{1,0},{2,3},{3,2},{4,5},{5,4},{6,7},{7,6},{8,9},{9,8},{10,11... | collective-permute-start | bytes 196616 | tf_op jit(solution)/shard_map/ppermute | solution.py:333
  52.9 0.0 collective-permute-start.14
  52.9 2.5 %collective-permute-done.17.refs_1_ = f32[1,128,128]{2,1,0:T(8,128)S(1)} collective-permute-done((f32[1,128,128]{2,1,0:T(8,128)S(1)}, f32[1,128,128]{2,1,0:T(8,128)S(1)}, u32[]{:S(2)}, u32[]{:S(2)}) %collective-permute-start.17) | collective-permute-done | bytes 65568 | tf_op jit(solution)/shard_map/ppermute | solution.py:333
  55.4 0.0 collective-permute-done.15.chip_in._
  55.5 3.8 %collective-permute-start.20 = (f32[2,128,128]{2,1,0:T(8,128)S(1)}, f32[2,128,128]{2,1,0:T(8,128)S(1)}, u32[]{:S(2)}, u32[]{:S(2)}) collective-permute-start(f32[2,128,128]{2,1,0:T(8,128)S(1)} %after.2.refs_0_), channel_id=1, source_target_pairs={{0,24},{4,28},{8,16},{12,20},{16,8},{20,12},{24,0},{28,4},{1,25},{... | collective-permute-start | bytes 393224 | tf_op jit(solution)/shard_map/ppermute | solution.py:333
  59.3 1.5 %collective-permute-start.19 = (f32[2,128,128]{2,1,0:T(8,128)S(1)}, f32[2,128,128]{2,1,0:T(8,128)S(1)}, u32[]{:S(2)}, u32[]{:S(2)}) collective-permute-start(f32[2,128,128]{2,1,0:T(8,128)S(1)} %after.2.refs_0_), channel_id=1, source_target_pairs={{0,8},{4,12},{8,0},{12,4},{16,24},{20,28},{24,16},{28,20},{1,9},{5... | collective-permute-start | bytes 393224 | tf_op jit(solution)/shard_map/ppermute | solution.py:333
  60.7 0.0 collective-permute-start.18
  60.8 0.0 collective-permute-done.14.core_in._
  60.8 2.4 %collective-permute-done.20.refs_3_ = f32[2,128,128]{2,1,0:T(8,128)S(1)} collective-permute-done((f32[2,128,128]{2,1,0:T(8,128)S(1)}, f32[2,128,128]{2,1,0:T(8,128)S(1)}, u32[]{:S(2)}, u32[]{:S(2)}) %collective-permute-start.20) | collective-permute-done | bytes 131104 | tf_op jit(solution)/shard_map/ppermute | solution.py:333
  63.2 2.0 %collective-permute-done.19.refs_2_ = f32[2,128,128]{2,1,0:T(8,128)S(1)} collective-permute-done((f32[2,128,128]{2,1,0:T(8,128)S(1)}, f32[2,128,128]{2,1,0:T(8,128)S(1)}, u32[]{:S(2)}, u32[]{:S(2)}) %collective-permute-start.19) | collective-permute-done | bytes 131104 | tf_op jit(solution)/shard_map/ppermute | solution.py:333
  65.2 1.3 %collective-permute-done.18.refs_1_ = f32[2,128,128]{2,1,0:T(8,128)S(1)} collective-permute-done((f32[2,128,128]{2,1,0:T(8,128)S(1)}, f32[2,128,128]{2,1,0:T(8,128)S(1)}, u32[]{:S(2)}, u32[]{:S(2)}) %collective-permute-start.18) | collective-permute-done | bytes 131104 | tf_op jit(solution)/shard_map/ppermute | solution.py:333
  66.5 0.1 collective-permute-start.21
  66.5 0.9 %columns.1 = f32[2,256,256]{2,1,0:T(8,128)} custom-call(f32[2,256,256]{2,1,0:T(8,128)S(1)} %get-tuple-element.23.inner_grad, f32[2,128,256]{2,1,0:T(8,128)S(1)} %collective-permute-done.14.core_in._, f32[2,128,256]{2,1,0:T(8,128)S(1)} %collective-permute-done.15.chip_in._), custom_call_target="tpu_custom_call" | custom-call | bytes 1572864 | tf_op jit(solution)/shard_map/columns/pallas_call | solution.py:398
  67.4 0.8 %join.1.refs_1_ = f32[2,2,256,256]{3,2,1,0:T(8,128)} custom-call(f32[8,128,128]{2,1,0:T(8,128)S(1)} %after.3.refs_0_), custom_call_target="tpu_custom_call" | custom-call | flops 2000000000 | bytes 1572864 | tf_op jit(solution)/shard_map/join/pallas_call | solution.py:398
  68.3 0.2 collective-permute-done.21.refs_0_
  68.4 0.8 %join_rest.1 = f32[2,2,256,256]{3,2,1,0:T(8,128)} custom-call(f32[8,128,128]{2,1,0:T(8,128)S(1)} %collective-permute-done.21.refs_0_, f32[2,2,256,256]{3,2,1,0:T(8,128)} %join.1.refs_1_), custom_call_target="tpu_custom_call", output_to_operand_aliasing={{}: (1, {})} | custom-call | bytes 2621440 | tf_op jit(solution)/shard_map/join_rest/pallas_call | solution.py:398
  (13 shorter events, 0.3 us)
Async XLA Ops:
  0.6 16.0 %collective-permute-start = (f32[2,256,256]{2,1,0:T(8,128)}, f32[2,256,256]{2,1,0:T(8,128)S(1)}, u32[]{:S(2)}, u32[]{:S(2)}) collective-permute-start(f32[2,256,256]{2,1,0:T(8,128)} %field.3), channel_id=1, source_target_pairs={{0,4},{4,0},{8,12},{12,8},{16,20},{20,16},{24,28},{28,24},{1,5},{5... | collective-permute-start | bytes 1572872 | tf_op jit(solution)/shard_map/ppermute | solution.py:363
  1.1 1.0 %copy-start.2 = (f32[2,256,256]{2,1,0:T(8,128)S(1)}, f32[2,256,256]{2,1,0:T(8,128)}, u32[]{:S(2)}) copy-start(f32[2,256,256]{2,1,0:T(8,128)} %field.3) | copy-start | bytes 1572868
  2.2 4.3 %copy-start.3 = (f32[1,1,3,256,256]{4,3,2,1,0:T(8,128)S(1)}, f32[1,1,3,256,256]{4,3,2,1,0:T(8,128)}, u32[]{:S(2)}) copy-start(f32[1,1,3,256,256]{4,3,2,1,0:T(8,128)} %param.8) | copy-start | bytes 2359300
  2.2 6.2 %collective-permute-start.1 = (f32[2,128,256]{2,1,0:T(8,128)S(1)}, f32[2,128,256]{2,1,0:T(8,128)S(1)}, u32[]{:S(2)}, u32[]{:S(2)}) collective-permute-start(f32[2,128,256]{2,1,0:T(8,128)S(1)} %chip_edges.1._), channel_id=1, source_target_pairs={{4,8},{8,4},{12,16},{16,12},{20,24},{24,20},{5,9},{9,5},{13,17},{1... | collective-permute-start | bytes 786440 | tf_op jit(solution)/shard_map/ppermute | solution.py:363
  3.2 10.4 %collective-permute-start.4 = (f32[2,256,128]{2,1,0:T(8,128)S(1)}, f32[2,256,128]{2,1,0:T(8,128)S(1)}, u32[]{:S(2)}, u32[]{:S(2)}) collective-permute-start(f32[2,256,128]{2,1,0:T(8,128)S(1)} %get-tuple-element.17), channel_id=1, source_target_pairs={{0,1},{1,0},{2,3},{3,2},{4,5},{5,4},{6,7},{7,6},{8,9},{9,8},{10,11... | collective-permute-start | bytes 786440 | tf_op jit(solution)/shard_map/ppermute | solution.py:363
  5.8 7.8 %collective-permute-start.5 = (f32[2,256,128]{2,1,0:T(8,128)S(1)}, f32[2,256,128]{2,1,0:T(8,128)S(1)}, u32[]{:S(2)}, u32[]{:S(2)}) collective-permute-start(f32[2,256,128]{2,1,0:T(8,128)S(1)} %get-tuple-element.18), channel_id=1, source_target_pairs={{1,2},{2,1},{5,6},{6,5},{9,10},{10,9},{13,14},{14,13},{17,18},{18,... | collective-permute-start | bytes 786440 | tf_op jit(solution)/shard_map/ppermute | solution.py:363
  6.5 0.7 copy-start.4
  6.5 0.7 copy-start.5
  8.5 8.1 %collective-permute-start.2 = (f32[2,128,128]{2,1,0:T(8,128)S(1)}, f32[2,128,128]{2,1,0:T(8,128)S(1)}, u32[]{:S(2)}, u32[]{:S(2)}) collective-permute-start(f32[2,128,128]{2,1,0:T(8,128)S(1)} %get-tuple-element.15), channel_id=1, source_target_pairs={{0,1},{1,0},{2,3},{3,2},{4,5},{5,4},{6,7},{7,6},{8,9},{9,8},{10,11... | collective-permute-start | bytes 393224 | tf_op jit(solution)/shard_map/ppermute | solution.py:363
  12.9 3.7 %collective-permute-start.3 = (f32[2,128,128]{2,1,0:T(8,128)S(1)}, f32[2,128,128]{2,1,0:T(8,128)S(1)}, u32[]{:S(2)}, u32[]{:S(2)}) collective-permute-start(f32[2,128,128]{2,1,0:T(8,128)S(1)} %get-tuple-element.16), channel_id=1, source_target_pairs={{1,2},{2,1},{5,6},{6,5},{9,10},{10,9},{13,14},{14,13},{17,18},{18,... | collective-permute-start | bytes 393224 | tf_op jit(solution)/shard_map/ppermute | solution.py:363
  13.6 4.1 %copy-start = (bf16[8,2,256,256]{3,2,1,0:T(8,128)(2,1)S(1)}, bf16[8,2,256,256]{3,2,1,0:T(8,128)(2,1)}, u32[]{:S(2)}) copy-start(bf16[8,2,256,256]{3,2,1,0:T(8,128)(2,1)} %constant.2.clone.tables) | copy-start | bytes 6291460
  13.6 4.1 %copy-start.1 = (f32[2,2,256,256]{3,2,1,0:T(8,128)S(1)}, f32[2,2,256,256]{3,2,1,0:T(8,128)}, u32[]{:S(2)}) copy-start(f32[2,2,256,256]{3,2,1,0:T(8,128)} %probe.1) | copy-start | bytes 3145732
  13.7 4.1 %collective-permute-start.6 = (f32[2,2,128,128]{3,2,1,0:T(8,128)S(1)}, f32[2,2,128,128]{3,2,1,0:T(8,128)S(1)}, u32[]{:S(2)}, u32[]{:S(2)}) collective-permute-start(f32[2,2,128,128]{3,2,1,0:T(8,128)S(1)} %near.1), channel_id=1, source_target_pairs={{0,4},{4,0},{8,12},{12,8},{16,20},{20,16},{24,28},{28,24},{1,5},{5... | collective-permute-start | bytes 786440 | tf_op jit(solution)/shard_map/ppermute | solution.py:363
  21.7 6.0 %collective-permute-start.9 = (f32[8,128,128]{2,1,0:T(8,128)S(1)}, f32[8,128,128]{2,1,0:T(8,128)S(1)}, u32[]{:S(2)}, u32[]{:S(2)}) collective-permute-start(f32[8,128,128]{2,1,0:T(8,128)S(1)} %slice.15), channel_id=1, source_target_pairs={{0,4},{4,0},{8,12},{12,8},{16,20},{20,16},{24,28},{28,24},{1,5},{5... | collective-permute-start | bytes 1572872 | tf_op jit(solution)/shard_map/ppermute | solution.py:363
  22.4 25.0 %collective-permute-start.7 = (f32[2,512,128]{2,1,0:T(8,128)S(1)}, f32[2,512,128]{2,1,0:T(8,128)S(1)}, u32[]{:S(2)}, u32[]{:S(2)}) collective-permute-start(f32[2,512,128]{2,1,0:T(8,128)S(1)} %get-tuple-element.20), channel_id=1, source_target_pairs={{0,1},{1,0},{2,3},{3,2},{4,5},{5,4},{6,7},{7,6},{8,9},{9,8},{10,11... | collective-permute-start | bytes 1572872 | tf_op jit(solution)/shard_map/ppermute | solution.py:363
  27.0 20.4 %collective-permute-start.8 = (f32[2,512,128]{2,1,0:T(8,128)S(1)}, f32[2,512,128]{2,1,0:T(8,128)S(1)}, u32[]{:S(2)}, u32[]{:S(2)}) collective-permute-start(f32[2,512,128]{2,1,0:T(8,128)S(1)} %get-tuple-element.21), channel_id=1, source_target_pairs={{1,2},{2,1},{5,6},{6,5},{9,10},{10,9},{13,14},{14,13},{17,18},{18,... | collective-permute-start | bytes 1572872 | tf_op jit(solution)/shard_map/ppermute | solution.py:363
  27.8 9.8 %collective-permute-start.12 = (f32[2,128,128]{2,1,0:T(8,128)S(1)}, f32[2,128,128]{2,1,0:T(8,128)S(1)}, u32[]{:S(2)}, u32[]{:S(2)}) collective-permute-start(f32[2,128,128]{2,1,0:T(8,128)S(1)} %get-tuple-element.26), channel_id=1, source_target_pairs={{0,24},{4,28},{8,16},{12,20},{16,8},{20,12},{24,0},{28,4},{1,25},{... | collective-permute-start | bytes 393224 | tf_op jit(solution)/shard_map/ppermute | solution.py:333
  33.3 5.9 %collective-permute-start.11 = (f32[2,128,128]{2,1,0:T(8,128)S(1)}, f32[2,128,128]{2,1,0:T(8,128)S(1)}, u32[]{:S(2)}, u32[]{:S(2)}) collective-permute-start(f32[2,128,128]{2,1,0:T(8,128)S(1)} %get-tuple-element.27), channel_id=1, source_target_pairs={{0,8},{4,12},{8,0},{12,4},{16,24},{20,28},{24,16},{28,20},{1,9},{5... | collective-permute-start | bytes 393224 | tf_op jit(solution)/shard_map/ppermute | solution.py:333
  33.3 6.6 %collective-permute-start.10 = (f32[2,128,128]{2,1,0:T(8,128)S(1)}, f32[2,128,128]{2,1,0:T(8,128)S(1)}, u32[]{:S(2)}, u32[]{:S(2)}) collective-permute-start(f32[2,128,128]{2,1,0:T(8,128)S(1)} %get-tuple-element.28), channel_id=1, source_target_pairs={{0,16},{4,20},{8,24},{12,28},{16,0},{20,4},{24,8},{28,12},{1,17},{... | collective-permute-start | bytes 393224 | tf_op jit(solution)/shard_map/ppermute | solution.py:333
  40.0 5.6 %collective-permute-start.13 = (f32[1,128,128]{2,1,0:T(8,128)S(1)}, f32[1,128,128]{2,1,0:T(8,128)S(1)}, u32[]{:S(2)}, u32[]{:S(2)}) collective-permute-start(f32[1,128,128]{2,1,0:T(8,128)S(1)} %slice.23), channel_id=1, source_target_pairs={{0,1},{1,0},{2,3},{3,2},{4,5},{5,4},{6,7},{7,6},{8,9},{9,8},{10,11... | collective-permute-start | bytes 196616 | tf_op jit(solution)/shard_map/ppermute | solution.py:333
  45.6 5.3 %collective-permute-start.16 = (f32[1,128,128]{2,1,0:T(8,128)S(1)}, f32[1,128,128]{2,1,0:T(8,128)S(1)}, u32[]{:S(2)}, u32[]{:S(2)}) collective-permute-start(f32[1,128,128]{2,1,0:T(8,128)S(1)} %add.6._.own), channel_id=1, source_target_pairs={{0,2},{1,3},{2,0},{3,1},{4,6},{5,7},{6,4},{7,5},{8,10},{9,11},{10,... | collective-permute-start | bytes 196616 | tf_op jit(solution)/shard_map/ppermute | solution.py:333
  47.5 7.9 %collective-permute-start.15 = (f32[2,128,256]{2,1,0:T(8,128)S(1)}, f32[2,128,256]{2,1,0:T(8,128)S(1)}, u32[]{:S(2)}, u32[]{:S(2)}) collective-permute-start(f32[2,128,256]{2,1,0:T(8,128)S(1)} %get-tuple-element.25), channel_id=1, source_target_pairs={{4,8},{8,4},{12,16},{16,12},{20,24},{24,20},{5,9},{9,5},{13,17},{1... | collective-permute-start | bytes 786440 | tf_op jit(solution)/shard_map/ppermute | solution.py:363
  50.9 4.6 %collective-permute-start.17 = (f32[1,128,128]{2,1,0:T(8,128)S(1)}, f32[1,128,128]{2,1,0:T(8,128)S(1)}, u32[]{:S(2)}, u32[]{:S(2)}) collective-permute-start(f32[1,128,128]{2,1,0:T(8,128)S(1)} %add.7.refs_0_), channel_id=1, source_target_pairs={{0,1},{1,0},{2,3},{3,2},{4,5},{5,4},{6,7},{7,6},{8,9},{9,8},{10,11... | collective-permute-start | bytes 196616 | tf_op jit(solution)/shard_map/ppermute | solution.py:333
  52.9 7.8 %collective-permute-start.14 = (f32[2,128,256]{2,1,0:T(8,128)S(1)}, f32[2,128,256]{2,1,0:T(8,128)S(1)}, u32[]{:S(2)}, u32[]{:S(2)}) collective-permute-start(f32[2,128,256]{2,1,0:T(8,128)S(1)} %get-tuple-element.24), channel_id=1, source_target_pairs={{0,4},{4,0},{8,12},{12,8},{16,20},{20,16},{24,28},{28,24},{1,5},{5... | collective-permute-start | bytes 786440 | tf_op jit(solution)/shard_map/ppermute | solution.py:363
  55.5 7.7 %collective-permute-start.20 = (f32[2,128,128]{2,1,0:T(8,128)S(1)}, f32[2,128,128]{2,1,0:T(8,128)S(1)}, u32[]{:S(2)}, u32[]{:S(2)}) collective-permute-start(f32[2,128,128]{2,1,0:T(8,128)S(1)} %after.2.refs_0_), channel_id=1, source_target_pairs={{0,24},{4,28},{8,16},{12,20},{16,8},{20,12},{24,0},{28,4},{1,25},{... | collective-permute-start | bytes 393224 | tf_op jit(solution)/shard_map/ppermute | solution.py:333
  59.3 5.9 %collective-permute-start.19 = (f32[2,128,128]{2,1,0:T(8,128)S(1)}, f32[2,128,128]{2,1,0:T(8,128)S(1)}, u32[]{:S(2)}, u32[]{:S(2)}) collective-permute-start(f32[2,128,128]{2,1,0:T(8,128)S(1)} %after.2.refs_0_), channel_id=1, source_target_pairs={{0,8},{4,12},{8,0},{12,4},{16,24},{20,28},{24,16},{28,20},{1,9},{5... | collective-permute-start | bytes 393224 | tf_op jit(solution)/shard_map/ppermute | solution.py:333
  60.7 5.7 %collective-permute-start.18 = (f32[2,128,128]{2,1,0:T(8,128)S(1)}, f32[2,128,128]{2,1,0:T(8,128)S(1)}, u32[]{:S(2)}, u32[]{:S(2)}) collective-permute-start(f32[2,128,128]{2,1,0:T(8,128)S(1)} %after.2.refs_0_), channel_id=1, source_target_pairs={{0,16},{4,20},{8,24},{12,28},{16,0},{20,4},{24,8},{28,12},{1,17},{... | collective-permute-start | bytes 393224 | tf_op jit(solution)/shard_map/ppermute | solution.py:333
  66.5 2.0 %collective-permute-start.21 = (f32[8,128,128]{2,1,0:T(8,128)S(1)}, f32[8,128,128]{2,1,0:T(8,128)S(1)}, u32[]{:S(2)}, u32[]{:S(2)}) collective-permute-start(f32[8,128,128]{2,1,0:T(8,128)S(1)} %after.3.refs_0_), channel_id=1, source_target_pairs={{0,4},{4,0},{8,12},{12,8},{16,20},{20,16},{24,28},{28,24},{1,5},{5... | collective-permute-start | bytes 1572872 | tf_op jit(solution)/shard_map/ppermute | solution.py:363
